TPU v7x, 256 devices: a whole 4x4x8 slice. The times are simulated.
256 devices in a mesh: dp: 4 (over y), ctx: 64 (over x, z, core).
Axes of the slice: x: 4, y: 4, z: 8, core: 2. Of those that a mesh axis runs over, the one named last changes fastest.
Arguments:
- queries: bfloat16 [4, 16384, 16, 128], P('dp', 'ctx'), may hold values from -64 to 64
- keys: bfloat16 [4, 16384, 8, 128], P('dp', 'ctx'), may hold values from -64 to 64
- values: bfloat16 [4, 16384, 8, 128], P('dp', 'ctx'), may hold values from -6 to 6
- out_grad: bfloat16 [4, 16384, 16, 128], P('dp', 'ctx'), may hold values from -8 to 8
- segment_ids: int32 [4, 16384], P('dp'), may hold values from 0 to 7, never falling along the last dimension, each value on 1 to 4096 neighbouring positions
- query_gain: float32 [128], replicated, may hold values from 0.5 to 6.5
- key_gain: float32 [128], replicated, may hold values from 0.5 to 6.5
Outputs:
- attention_out: bfloat16 [4, 16384, 16, 128], P('dp', 'ctx')
- query_grad: bfloat16 [4, 16384, 16, 128], P('dp', 'ctx')
- key_grad: bfloat16 [4, 16384, 8, 128], P('dp', 'ctx')
- value_grad: bfloat16 [4, 16384, 8, 128], P('dp', 'ctx')
- query_gain_grad: float32 [128], replicated
- key_gain_grad: float32 [128], replicated
All inputs are finite; a program needn't handle non-finite values.
Results may differ from a plain program's by a relative error of at most 0.034.
The roundings to bfloat16 on the way count: a program that leaves them out, or rounds other values in their place, can miss the bound.
Values may be sent and summed in bfloat16 or wider, within the bound.
A program may use at most 128 MiB of HBM per device.

v0:
```python
import jax
import jax.numpy as jnp
from jax import lax
from jax.sharding import PartitionSpec as P

LOOKBACK_TOKENS = 1024


score_scale = 168.0 ** (-0.5)
eps = 1e-06


def from_behind(value, axis, steps):
    count = lax.axis_size(axis)
    initial, last = (max(0, -steps), min(count, count - steps))
    return lax.ppermute(value, axis, [(source, source + steps) for source in range(initial, last)])


def normalize(unscaled_scores, gain):
    values = unscaled_scores.astype(jnp.float32)
    factor = lax.rsqrt(jnp.mean(values * values, axis=-1, keepdims=True) + eps)
    unit = values * factor
    return (unit, factor, (unit * gain).astype(jnp.bfloat16))


def norm_backward(grad, unit, factor, gain):
    scaled = grad * gain
    inner = jnp.mean(scaled * unit, axis=-1, keepdims=True)
    return (
        (factor * (scaled - unit * inner)).astype(jnp.bfloat16),
        jnp.sum(grad * unit, axis=(0, 1)),
    )


def group_block(query_group, key_rows, value_rows, grad_group, allowed):
    wide = jnp.float32
    scores = (
        jnp.einsum("tgqc,kgc->gqtk", query_group, key_rows, preferred_element_type=wide)
        * score_scale
    )
    scores = jnp.where(allowed[None, None], scores, -jnp.inf)
    top = jnp.max(scores, axis=-1, keepdims=True)
    lse = top + jnp.log(jnp.sum(jnp.exp(scores - top), axis=-1, keepdims=True))
    probs = jnp.exp(scores - lse)
    rounded = probs.astype(jnp.bfloat16)
    output = jnp.einsum("gqtk,kgc->tgqc", rounded, value_rows, preferred_element_type=wide).astype(
        jnp.bfloat16
    )
    dprob = jnp.einsum("tgqc,kgc->gqtk", grad_group, value_rows, preferred_element_type=wide)
    delta = jnp.einsum("tgqc,tgqc->gqt", grad_group, output, preferred_element_type=wide)
    dscore = (probs * (dprob - delta[..., None])).astype(jnp.bfloat16)
    dquery = (
        jnp.einsum("gqtk,kgc->tgqc", dscore, key_rows, preferred_element_type=wide) * score_scale
    )
    dkey = (
        jnp.einsum("gqtk,tgqc->kgc", dscore, query_group, preferred_element_type=wide) * score_scale
    )
    dvalue = jnp.einsum("gqtk,tgqc->kgc", rounded, grad_group, preferred_element_type=wide)
    return (output, dquery, dkey, dvalue)


def local(queries, keys, values, out_grad, segment_ids, query_gain, key_gain):
    tokens = queries.shape[1]
    heads = queries.shape[2]
    kv_heads = keys.shape[2]
    width = queries.shape[3]
    query_cluster = heads // kv_heads
    span = LOOKBACK_TOKENS // tokens
    position = lax.axis_index("ctx")
    query_unit, query_factor, normalized_query = normalize(queries[0], query_gain)
    key_unit, key_factor, normalized_key = normalize(keys[0], key_gain)
    value_rows = values[0]
    earlier = [from_behind((normalized_key, value_rows), "ctx", hop) for hop in range(span, 0, -1)]
    key_all = jnp.concatenate([piece[0] for piece in earlier] + [normalized_key], axis=0)
    value_all = jnp.concatenate([piece[1] for piece in earlier] + [value_rows], axis=0)
    total = key_all.shape[0]
    segments = segment_ids[0]
    seg_padded = jnp.concatenate([jnp.full((span * tokens,), -1, jnp.int32), segments], axis=0)
    seg_query = lax.dynamic_slice_in_dim(segments, position * tokens, tokens, 0)
    seg_key = lax.dynamic_slice_in_dim(seg_padded, position * tokens, total, 0)
    offset = (
        jnp.arange(tokens, dtype=jnp.int32)[:, None]
        + span * tokens
        - jnp.arange(total, dtype=jnp.int32)[None, :]
    )
    allowed = (offset >= 0) & (offset < LOOKBACK_TOKENS) & (seg_query[:, None] == seg_key[None, :])
    query_groups = normalized_query.reshape(tokens, kv_heads, query_cluster, width)
    grad_groups = out_grad[0].reshape(tokens, kv_heads, query_cluster, width)
    portions = 2
    group_width = kv_heads // portions
    pieces = []
    for portion in range(portions):
        first = portion * group_width
        last = first + group_width
        pieces.append(
            group_block(
                query_groups[:, first:last],
                key_all[:, first:last],
                value_all[:, first:last],
                grad_groups[:, first:last],
                allowed,
            )
        )
    output = jnp.concatenate([piece[0] for piece in pieces], axis=1).reshape(tokens, heads, width)
    dquery_normed = jnp.concatenate([piece[1] for piece in pieces], axis=1).reshape(
        tokens, heads, width
    )
    dkey_blocks = jnp.concatenate([piece[2] for piece in pieces], axis=1).reshape(
        span + 1, tokens, kv_heads, width
    )
    dvalue_blocks = jnp.concatenate([piece[3] for piece in pieces], axis=1).reshape(
        span + 1, tokens, kv_heads, width
    )
    dkey_sum = dkey_blocks[span]
    dvalue_sum = dvalue_blocks[span]
    for hop in range(1, span + 1):
        outgoing = (
            dkey_blocks[span - hop].astype(jnp.bfloat16),
            dvalue_blocks[span - hop].astype(jnp.bfloat16),
        )
        arrived = from_behind((outgoing[0], outgoing[1]), "ctx", -hop)
        dkey_sum = dkey_sum + arrived[0].astype(jnp.float32)
        dvalue_sum = dvalue_sum + arrived[1].astype(jnp.float32)
    query_grad, query_part = norm_backward(dquery_normed, query_unit, query_factor, query_gain)
    key_grad, key_part = norm_backward(dkey_sum, key_unit, key_factor, key_gain)
    query_total, key_total = lax.psum((query_part, key_part), ("dp", "ctx"))
    return (
        output[None],
        query_grad[None],
        key_grad[None],
        dvalue_sum.astype(jnp.bfloat16)[None],
        query_total,
        key_total,
    )


def solution(mesh):
    in_specs = (
        P("dp", "ctx", None, None),
        P("dp", "ctx", None, None),
        P("dp", "ctx", None, None),
        P("dp", "ctx", None, None),
        P("dp", None),
        P(),
        P(),
    )
    out_specs = (
        P("dp", "ctx", None, None),
        P("dp", "ctx", None, None),
        P("dp", "ctx", None, None),
        P("dp", "ctx", None, None),
        P(),
        P(),
    )
    return jax.shard_map(local, mesh=mesh, in_specs=in_specs, out_specs=out_specs, check_vma=False)
```

profile of v0, /device:TPU:1, one launch (start us, length us, event | category | flops | bytes accessed | tf_op | source)
XLA Modules:
  0.0 389.4 jit_solution(11055309058896009378)
XLA Ops:
  4.3 4.9 %collective-permute-start.7 = (bf16[256,8,128]{2,0,1:T(8,128)(2,1)}, bf16[256,8,128]{2,0,1:T(8,128)(2,1)}, u32[]{:S(2)}, u32[]{:S(2)}) collective-permute-start(bf16[256,8,128]{2,0,1:T(8,128)(2,1)} %fusion.34), channel_id=1, source_target_pairs={{0,1},{1,2},{2,3},{3,4},{4,5},{5,6},{6,7},{7,8},{8,9},{9,10},{10,1... | collective-permute-start | bytes 1572872 | tf_op jit(solution)/shard_map/ppermute | solution.py:16
  9.3 4.3 %collective-permute-start.6 = (bf16[256,8,128]{2,0,1:T(8,128)(2,1)}, bf16[256,8,128]{2,0,1:T(8,128)(2,1)}, u32[]{:S(2)}, u32[]{:S(2)}) collective-permute-start(bf16[256,8,128]{2,0,1:T(8,128)(2,1)} %fusion.34), channel_id=1, source_target_pairs={{0,2},{1,3},{2,4},{3,5},{4,6},{5,7},{6,8},{7,9},{8,10},{9,11},{10,... | collective-permute-start | bytes 1572872 | tf_op jit(solution)/shard_map/ppermute | solution.py:16
  13.6 3.6 collective-permute-start.5
  17.2 5.2 %collective-permute-start.4 = (bf16[256,8,128]{2,0,1:T(8,128)(2,1)}, bf16[256,8,128]{2,0,1:T(8,128)(2,1)}, u32[]{:S(2)}, u32[]{:S(2)}) collective-permute-start(bf16[256,8,128]{2,0,1:T(8,128)(2,1)} %fusion.34), channel_id=1, source_target_pairs={{0,4},{1,5},{2,6},{3,7},{4,8},{5,9},{6,10},{7,11},{8,12},{9,13},{1... | collective-permute-start | bytes 1572872 | tf_op jit(solution)/shard_map/ppermute | solution.py:16
  24.6 3.2 collective-permute-start
  32.9 24.1 %collective-permute-done.4 = bf16[256,8,128]{2,0,1:T(8,128)(2,1)} collective-permute-done((bf16[256,8,128]{2,0,1:T(8,128)(2,1)}, bf16[256,8,128]{2,0,1:T(8,128)(2,1)}, u32[]{:S(2)}, u32[]{:S(2)}) %collective-permute-start.4) | collective-permute-done | bytes 524320 | tf_op jit(solution)/shard_map/ppermute | solution.py:16
  57.0 21.3 %collective-permute-start.3 = (bf16[256,8,128]{0,2,1:T(8,128)(2,1)}, bf16[256,8,128]{0,2,1:T(8,128)(2,1)S(1)}, u32[]{:S(2)}, u32[]{:S(2)}) collective-permute-start(bf16[256,8,128]{0,2,1:T(8,128)(2,1)} %bitcast.4), channel_id=1, source_target_pairs={{0,1},{1,2},{2,3},{3,4},{4,5},{5,6},{6,7},{7,8},{8,9},{9,10},{10,1... | collective-permute-start | bytes 1572872 | tf_op jit(solution)/shard_map/ppermute | solution.py:16
  79.4 12.9 %collective-permute-start.2 = (bf16[256,8,128]{0,2,1:T(8,128)(2,1)}, bf16[256,8,128]{0,2,1:T(8,128)(2,1)S(1)}, u32[]{:S(2)}, u32[]{:S(2)}) collective-permute-start(bf16[256,8,128]{0,2,1:T(8,128)(2,1)} %bitcast.4), channel_id=1, source_target_pairs={{0,2},{1,3},{2,4},{3,5},{4,6},{5,7},{6,8},{7,9},{8,10},{9,11},{10,... | collective-permute-start | bytes 1572872 | tf_op jit(solution)/shard_map/ppermute | solution.py:16
  93.5 3.6 collective-permute-start.1
  100.9 24.6 %collective-permute-done.1 = bf16[256,8,128]{0,2,1:T(8,128)(2,1)S(1)} collective-permute-done((bf16[256,8,128]{0,2,1:T(8,128)(2,1)}, bf16[256,8,128]{0,2,1:T(8,128)(2,1)S(1)}, u32[]{:S(2)}, u32[]{:S(2)}) %collective-permute-start.1) | collective-permute-done | bytes 524320 | tf_op jit(solution)/shard_map/ppermute | solution.py:16
  127.3 6.1 %fusion.66 = (f32[4,2,256]{2,1,0:T(2,128)S(1)}, f32[4,2,256,1280]{2,3,1,0:T(8,128)}) fusion(bf16[256,8,2,128]{3,0,2,1:T(8,128)(2,1)S(1)} %copy-done.10, bf16[1280,8,128]{2,0,1:T(8,128)(2,1)S(1)} %constant_dynamic-update-slice_fusion.5, pred[256,1280]{0,1:T(8,128)(4,1)S(1)} %copy-done.17), kind=kOutput, calls=%fused_computation.114 | convolution fusion | flops 678950912 | bytes 12656640 | tf_op jit(solution)/shard_map/tgqc,kgc->gqtk/dot_general | solution.py:38
  136.3 3.0 bitcast_convert_fusion
  141.9 7.2 %convolution_bitcast_fusion.2 = f32[1280,4,128]{2,0,1:T(8,128)} fusion(f32[4,2,256,1280]{2,3,1,0:T(8,128)} %copy-done, f32[4,2,256]{2,1,0:T(2,128)S(1)} %bitcast.150, bf16[256,8,2,128]{3,0,2,1:T(8,128)(2,1)} %bitcast.139), kind=kOutput, calls=%fused_computation.28 | convolution fusion | flops 676331520 | bytes 13639680 | tf_op jit(solution)/shard_map/gqtk,tgqc->kgc/dot_general | solution.py:58
  151.4 3.1 bitcast_convert_fusion.1
  159.9 5.5 %fusion.1 = bf16[4,2,256,1280]{2,3,1,0:T(8,128)(2,1)S(1)} fusion(f32[4,2,256,1280]{2,3,1,0:T(8,128)} %copy-done, f32[4,2,256]{2,1,0:T(2,128)S(1)} %get-tuple-element.29, f32[4,2,256]{2,1,0:T(2,128)S(1)} %bitcast.151, bf16[1280,8,128]{0,2,1:T(8,128)(2,1)S(1)} %constant_dynamic-update-slice_fusion, bf16[256,8,2,128]{3,0,2,1:T(8,128)(2,1)S(1)} %bitcast.141), kind=kOutput, calls=%fused_computation.2 | convolution fusion | flops 681574400 | bytes 17580032 | tf_op jit(solution)/shard_map/tgqc,kgc->gqtk/dot_general | solution.py:49
  167.4 3.1 fusion.9
  170.5 3.1 convolution_bitcast_fusion.3
  178.2 3.0 fusion.11
  203.8 3.7 collective-permute-done.8
  208.8 13.7 %collective-permute-done.11 = bf16[256,8,128]{2,0,1:T(8,128)(2,1)S(1)} collective-permute-done((bf16[256,8,128]{2,0,1:T(8,128)(2,1)S(1)}, bf16[256,8,128]{2,0,1:T(8,128)(2,1)S(1)}, u32[]{:S(2)}, u32[]{:S(2)}) %collective-permute-start.11) | collective-permute-done | bytes 524320 | tf_op jit(solution)/shard_map/ppermute | solution.py:16
  223.8 24.2 %collective-permute-done.10 = bf16[256,8,128]{2,0,1:T(8,128)(2,1)S(1)} collective-permute-done((bf16[256,8,128]{2,0,1:T(8,128)(2,1)S(1)}, bf16[256,8,128]{2,0,1:T(8,128)(2,1)S(1)}, u32[]{:S(2)}, u32[]{:S(2)}) %collective-permute-start.10) | collective-permute-done | bytes 524320 | tf_op jit(solution)/shard_map/ppermute | solution.py:16
  252.0 15.6 %collective-permute-done.15 = bf16[256,8,128]{2,0,1:T(8,128)(2,1)S(1)} collective-permute-done((bf16[256,8,128]{2,0,1:T(8,128)(2,1)S(1)}, bf16[256,8,128]{2,0,1:T(8,128)(2,1)S(1)}, u32[]{:S(2)}, u32[]{:S(2)}) %collective-permute-start.15) | collective-permute-done | bytes 524320 | tf_op jit(solution)/shard_map/ppermute | solution.py:16
  267.6 37.9 %collective-permute-done.14 = bf16[256,8,128]{2,0,1:T(8,128)(2,1)S(1)} collective-permute-done((bf16[256,8,128]{2,0,1:T(8,128)(2,1)S(1)}, bf16[256,8,128]{2,0,1:T(8,128)(2,1)S(1)}, u32[]{:S(2)}, u32[]{:S(2)}) %collective-permute-start.14) | collective-permute-done | bytes 524320 | tf_op jit(solution)/shard_map/ppermute | solution.py:16
  307.0 82.4 %all-reduce.1 = (f32[128]{0:T(128)}, f32[128]{0:T(128)}) all-reduce(f32[128]{0:T(128)S(1)} %get-tuple-element.24, f32[128]{0:T(128)S(1)} %get-tuple-element.26), channel_id=1, replica_groups=mesh['dp'=4,'ctx'=64] {'dp','ctx'}, use_global_device_ids=true, to_apply=%region_9.10 | all-reduce | flops 256 | bytes 2048 | tf_op jit(solution)/shard_map/psum | solution.py:126
  (129 shorter events, 68.7 us)
Async XLA Ops:
  0.6 27.1 %copy-start.7 = (bf16[1,256,16,128]{3,2,1,0:T(8,128)(2,1)S(1)}, bf16[1,256,16,128]{3,2,1,0:T(8,128)(2,1)}, u32[]{:S(2)}) copy-start(bf16[1,256,16,128]{3,2,1,0:T(8,128)(2,1)} %param.7) | copy-start | bytes 3145732
  0.6 27.8 %copy-start.18 = (s32[1,16384]{1,0:T(1,128)S(1)}, s32[1,16384]{1,0:T(1,128)}, u32[]{:S(2)}) copy-start(s32[1,16384]{1,0:T(1,128)} %param.11) | copy-start | bytes 196612
  4.3 94.9 %collective-permute-start.7 = (bf16[256,8,128]{2,0,1:T(8,128)(2,1)}, bf16[256,8,128]{2,0,1:T(8,128)(2,1)}, u32[]{:S(2)}, u32[]{:S(2)}) collective-permute-start(bf16[256,8,128]{2,0,1:T(8,128)(2,1)} %fusion.34), channel_id=1, source_target_pairs={{0,1},{1,2},{2,3},{3,4},{4,5},{5,6},{6,7},{7,8},{8,9},{9,10},{10,1... | collective-permute-start | bytes 1572872 | tf_op jit(solution)/shard_map/ppermute | solution.py:16
  9.3 88.9 %collective-permute-start.6 = (bf16[256,8,128]{2,0,1:T(8,128)(2,1)}, bf16[256,8,128]{2,0,1:T(8,128)(2,1)}, u32[]{:S(2)}, u32[]{:S(2)}) collective-permute-start(bf16[256,8,128]{2,0,1:T(8,128)(2,1)} %fusion.34), channel_id=1, source_target_pairs={{0,2},{1,3},{2,4},{3,5},{4,6},{5,7},{6,8},{7,9},{8,10},{9,11},{10,... | collective-permute-start | bytes 1572872 | tf_op jit(solution)/shard_map/ppermute | solution.py:16
  13.6 79.8 %collective-permute-start.5 = (bf16[256,8,128]{2,0,1:T(8,128)(2,1)}, bf16[256,8,128]{2,0,1:T(8,128)(2,1)}, u32[]{:S(2)}, u32[]{:S(2)}) collective-permute-start(bf16[256,8,128]{2,0,1:T(8,128)(2,1)} %fusion.34), channel_id=1, source_target_pairs={{0,3},{1,4},{2,5},{3,6},{4,7},{5,8},{6,9},{7,10},{8,11},{9,12},{10... | collective-permute-start | bytes 1572872 | tf_op jit(solution)/shard_map/ppermute | solution.py:16
  17.2 39.8 %collective-permute-start.4 = (bf16[256,8,128]{2,0,1:T(8,128)(2,1)}, bf16[256,8,128]{2,0,1:T(8,128)(2,1)}, u32[]{:S(2)}, u32[]{:S(2)}) collective-permute-start(bf16[256,8,128]{2,0,1:T(8,128)(2,1)} %fusion.34), channel_id=1, source_target_pairs={{0,4},{1,5},{2,6},{3,7},{4,8},{5,9},{6,10},{7,11},{8,12},{9,13},{1... | collective-permute-start | bytes 1572872 | tf_op jit(solution)/shard_map/ppermute | solution.py:16
  24.6 54.8 %collective-permute-start = (bf16[256,8,128]{0,2,1:T(8,128)(2,1)}, bf16[256,8,128]{0,2,1:T(8,128)(2,1)}, u32[]{:S(2)}, u32[]{:S(2)}) collective-permute-start(bf16[256,8,128]{0,2,1:T(8,128)(2,1)} %bitcast.4), channel_id=1, source_target_pairs={{0,4},{1,5},{2,6},{3,7},{4,8},{5,9},{6,10},{7,11},{8,12},{9,13},{1... | collective-permute-start | bytes 1572872 | tf_op jit(solution)/shard_map/ppermute | solution.py:16
  32.9 67.5 %copy-start.9 = (bf16[1,256,8,128]{3,2,1,0:T(8,128)(2,1)S(1)}, bf16[1,256,8,128]{3,2,1,0:T(8,128)(2,1)}, u32[]{:S(2)}) copy-start(bf16[1,256,8,128]{3,2,1,0:T(8,128)(2,1)} %param.8) | copy-start | bytes 1572868
  32.9 67.5 %copy-start.19 = (f32[128]{0:T(128)S(1)}, f32[128]{0:T(128)}, u32[]{:S(2)}) copy-start(f32[128]{0:T(128)} %param.13) | copy-start | bytes 1540
  57.0 76.4 %collective-permute-start.3 = (bf16[256,8,128]{0,2,1:T(8,128)(2,1)}, bf16[256,8,128]{0,2,1:T(8,128)(2,1)S(1)}, u32[]{:S(2)}, u32[]{:S(2)}) collective-permute-start(bf16[256,8,128]{0,2,1:T(8,128)(2,1)} %bitcast.4), channel_id=1, source_target_pairs={{0,1},{1,2},{2,3},{3,4},{4,5},{5,6},{6,7},{7,8},{8,9},{9,10},{10,1... | collective-permute-start | bytes 1572872 | tf_op jit(solution)/shard_map/ppermute | solution.py:16
  79.4 47.8 %collective-permute-start.2 = (bf16[256,8,128]{0,2,1:T(8,128)(2,1)}, bf16[256,8,128]{0,2,1:T(8,128)(2,1)S(1)}, u32[]{:S(2)}, u32[]{:S(2)}) collective-permute-start(bf16[256,8,128]{0,2,1:T(8,128)(2,1)} %bitcast.4), channel_id=1, source_target_pairs={{0,2},{1,3},{2,4},{3,5},{4,6},{5,7},{6,8},{7,9},{8,10},{9,11},{10,... | collective-permute-start | bytes 1572872 | tf_op jit(solution)/shard_map/ppermute | solution.py:16
  93.4 32.2 %copy-start.10 = (bf16[256,8,2,128]{3,0,2,1:T(8,128)(2,1)S(1)}, bf16[256,8,2,128]{3,0,2,1:T(8,128)(2,1)}, u32[]{:S(2)}) copy-start(bf16[256,8,2,128]{3,0,2,1:T(8,128)(2,1)} %multiply_convert_fusion.1) | copy-start | bytes 3145732
  93.4 32.2 %copy-start.17 = (pred[256,1280]{0,1:T(8,128)(4,1)S(1)}, pred[256,1280]{0,1:T(8,128)(4,1)}, u32[]{:S(2)}) copy-start(pred[256,1280]{0,1:T(8,128)(4,1)} %fusion.27) | copy-start | bytes 983044
  93.5 32.1 %collective-permute-start.1 = (bf16[256,8,128]{0,2,1:T(8,128)(2,1)}, bf16[256,8,128]{0,2,1:T(8,128)(2,1)S(1)}, u32[]{:S(2)}, u32[]{:S(2)}) collective-permute-start(bf16[256,8,128]{0,2,1:T(8,128)(2,1)} %bitcast.4), channel_id=1, source_target_pairs={{0,3},{1,4},{2,5},{3,6},{4,7},{5,8},{6,9},{7,10},{8,11},{9,12},{10... | collective-permute-start | bytes 1572872 | tf_op jit(solution)/shard_map/ppermute | solution.py:16
  100.9 26.4 %copy-start.12 = (bf16[1280,8,128]{2,0,1:T(8,128)(2,1)}, bf16[1280,8,128]{2,0,1:T(8,128)(2,1)S(1)}, u32[]{:S(2)}) copy-start(bf16[1280,8,128]{2,0,1:T(8,128)(2,1)S(1)} %constant_dynamic-update-slice_fusion.5) | copy-start | bytes 7864324
  192.3 15.3 %collective-permute-start.8 = (bf16[256,8,128]{2,0,1:T(8,128)(2,1)S(1)}, bf16[256,8,128]{2,0,1:T(8,128)(2,1)S(1)}, u32[]{:S(2)}, u32[]{:S(2)}) collective-permute-start(bf16[256,8,128]{2,0,1:T(8,128)(2,1)S(1)} %get-tuple-element.37), channel_id=1, source_target_pairs={{1,0},{2,1},{3,2},{4,3},{5,4},{6,5},{7,6},{8,7},{9,8},{10,9},{11,1... | collective-permute-start | bytes 1572872 | tf_op jit(solution)/shard_map/ppermute | solution.py:16
  194.3 28.2 %collective-permute-start.11 = (bf16[256,8,128]{2,0,1:T(8,128)(2,1)S(1)}, bf16[256,8,128]{2,0,1:T(8,128)(2,1)S(1)}, u32[]{:S(2)}, u32[]{:S(2)}) collective-permute-start(bf16[256,8,128]{2,0,1:T(8,128)(2,1)S(1)} %get-tuple-element.38), channel_id=1, source_target_pairs={{4,0},{5,1},{6,2},{7,3},{8,4},{9,5},{10,6},{11,7},{12,8},{13,9},{1... | collective-permute-start | bytes 1572872 | tf_op jit(solution)/shard_map/ppermute | solution.py:16
  195.6 52.4 %collective-permute-start.10 = (bf16[256,8,128]{2,0,1:T(8,128)(2,1)S(1)}, bf16[256,8,128]{2,0,1:T(8,128)(2,1)S(1)}, u32[]{:S(2)}, u32[]{:S(2)}) collective-permute-start(bf16[256,8,128]{2,0,1:T(8,128)(2,1)S(1)} %get-tuple-element.39), channel_id=1, source_target_pairs={{3,0},{4,1},{5,2},{6,3},{7,4},{8,5},{9,6},{10,7},{11,8},{12,9},{13... | collective-permute-start | bytes 1572872 | tf_op jit(solution)/shard_map/ppermute | solution.py:16
  196.9 52.4 %collective-permute-start.9 = (bf16[256,8,128]{2,0,1:T(8,128)(2,1)S(1)}, bf16[256,8,128]{2,0,1:T(8,128)(2,1)S(1)}, u32[]{:S(2)}, u32[]{:S(2)}) collective-permute-start(bf16[256,8,128]{2,0,1:T(8,128)(2,1)S(1)} %get-tuple-element.40), channel_id=1, source_target_pairs={{2,0},{3,1},{4,2},{5,3},{6,4},{7,5},{8,6},{9,7},{10,8},{11,9},{12,... | collective-permute-start | bytes 1572872 | tf_op jit(solution)/shard_map/ppermute | solution.py:16
  199.1 50.2 %copy-start.3 = (f32[1280,4,128]{2,0,1:T(8,128)S(1)}, f32[1280,4,128]{2,0,1:T(8,128)}, u32[]{:S(2)}) copy-start(f32[1280,4,128]{2,0,1:T(8,128)} %fusion.11) | copy-start | bytes 7864324
  199.1 53.0 %collective-permute-start.12 = (bf16[256,8,128]{2,0,1:T(8,128)(2,1)S(1)}, bf16[256,8,128]{2,0,1:T(8,128)(2,1)S(1)}, u32[]{:S(2)}, u32[]{:S(2)}) collective-permute-start(bf16[256,8,128]{2,0,1:T(8,128)(2,1)S(1)} %get-tuple-element.33), channel_id=1, source_target_pairs={{1,0},{2,1},{3,2},{4,3},{5,4},{6,5},{7,6},{8,7},{9,8},{10,9},{11,1... | collective-permute-start | bytes 1572872 | tf_op jit(solution)/shard_map/ppermute | solution.py:16
  207.6 60.1 %collective-permute-start.15 = (bf16[256,8,128]{2,0,1:T(8,128)(2,1)S(1)}, bf16[256,8,128]{2,0,1:T(8,128)(2,1)S(1)}, u32[]{:S(2)}, u32[]{:S(2)}) collective-permute-start(bf16[256,8,128]{2,0,1:T(8,128)(2,1)S(1)} %get-tuple-element.34), channel_id=1, source_target_pairs={{4,0},{5,1},{6,2},{7,3},{8,4},{9,5},{10,6},{11,7},{12,8},{13,9},{1... | collective-permute-start | bytes 1572872 | tf_op jit(solution)/shard_map/ppermute | solution.py:16
  222.5 83.0 %collective-permute-start.14 = (bf16[256,8,128]{2,0,1:T(8,128)(2,1)S(1)}, bf16[256,8,128]{2,0,1:T(8,128)(2,1)S(1)}, u32[]{:S(2)}, u32[]{:S(2)}) collective-permute-start(bf16[256,8,128]{2,0,1:T(8,128)(2,1)S(1)} %get-tuple-element.35), channel_id=1, source_target_pairs={{3,0},{4,1},{5,2},{6,3},{7,4},{8,5},{9,6},{10,7},{11,8},{12,9},{13... | collective-permute-start | bytes 1572872 | tf_op jit(solution)/shard_map/ppermute | solution.py:16
  248.0 57.6 %collective-permute-start.13 = (bf16[256,8,128]{2,0,1:T(8,128)(2,1)S(1)}, bf16[256,8,128]{2,0,1:T(8,128)(2,1)S(1)}, u32[]{:S(2)}, u32[]{:S(2)}) collective-permute-start(bf16[256,8,128]{2,0,1:T(8,128)(2,1)S(1)} %get-tuple-element.36), channel_id=1, source_target_pairs={{2,0},{3,1},{4,2},{5,3},{6,4},{7,5},{8,6},{9,7},{10,8},{11,9},{12,... | collective-permute-start | bytes 1572872 | tf_op jit(solution)/shard_map/ppermute | solution.py:16
  (19 other events, 104.5 us)
where the time goes:
time: 391 us; the launch traced here: 389 us
  waiting for transfers between devices  144 us (37%)
  blocking collectives  82.4 us (21%)
  starting transfers between devices  71.3 us (18%)
  matrix products  42.3 us (11%)
  other arithmetic  24.6 us (6%)
  local copies, waits for them, and re-layouts  23.7 us (6%)
    ppermute x16, waiting for transfers between devices, from_behind(): lax.ppermute(value, axis, [(source, source + steps) for source in range(i...  144 us
    psum x1, blocking collectives, local(): query_total, key_total = lax.psum((query_part, key_part), ('dp', 'ctx'))  82.4 us
    ppermute x16, starting transfers between devices, from_behind(): lax.ppermute(value, axis, [(source, source + steps) for source in range(i...  71.3 us
    unnamed x69, local copies, waits for them, and re-layouts  19.2 us
    dot_general x2, matrix products, group_block(): jnp.einsum('gqtk,tgqc->kgc', rounded, grad_group, preferred_element_type=...  10.3 us
    dot_general x2, matrix products, group_block(): jnp.einsum('tgqc,kgc->gqtk', grad_group, value_rows, preferred_element_ty...  8.21 us
  transfers between devices with their start and end apart: 16, of which 7 were waited for; matrix products, arithmetic and copies ran while one was open for 7% of the time, Pallas kernels for 0%

commit v1 on v0

v1 whole, which is shorter than its diff:
```python
import jax
import jax.numpy as jnp
from jax import lax
from jax.experimental import pallas as pl
from jax.experimental.pallas import tpu as pltpu
from jax.sharding import PartitionSpec as P

LOOKBACK_TOKENS = 1024
BLOCK = 256
WIDTH = 128
SPAN = 6
score_scale = 168.0 ** (-0.5)
log2_scale = score_scale * 1.4426950408889634
eps = 1e-06
HIDDEN = -1e30
AHEAD = 3

MESH = pl.DeviceIdType.MESH
NT = (((1,), (1,)), ((), ()))
TN = (((0,), (0,)), ((), ()))
NN = (((1,), (0,)), ((), ()))


def dot(a, b, dims):
    return lax.dot_general(a, b, dims, preferred_element_type=jnp.float32)


def rows(block):
    return pl.ds(pl.multiple_of(block * BLOCK, BLOCK), BLOCK)


def normalize(raw, gain):
    wide = raw.astype(jnp.float32)
    factor = lax.rsqrt(jnp.mean(wide * wide, axis=-1, keepdims=True) + eps)
    unit = wide * factor
    return unit, factor, (unit * gain).astype(jnp.bfloat16)


def norm_backward(grad, unit, factor, gain):
    scaled = grad * gain
    inner = jnp.mean(scaled * unit, axis=-1, keepdims=True)
    return (factor * (scaled - unit * inner)).astype(jnp.bfloat16), jnp.sum(
        grad * unit, axis=0, keepdims=True
    )


def kernel(
    q_ref, k_ref, v_ref, g_ref, seg_key, seg_query, gain_ref,
    o_ref, dq_ref, dk_ref, dv_ref, part_ref,
    kv, q_all, g_all, mask, s_buf, d_buf, p_bf, ds_bf, o_buf, dq_buf,
    held, pair_out, pair_in, a_out, a_in, b_out, b_in,
    one_send, one_recv, sends, recvs,
):
    dp = lax.axis_index("dp")
    me = lax.axis_index("ctx")
    count = lax.axis_size("ctx")
    core = lax.rem(me, 2)
    other = 1 - core
    sibling = (dp, me + 1 - 2 * core)
    after = (dp, lax.rem(me + 2, count))
    before = (dp, lax.rem(me + count - 2, count))
    heads = k_ref.shape[0]

    def remote(src, dst, kind, head, device):
        return pltpu.make_async_remote_copy(
            src_ref=src, dst_ref=dst, send_sem=sends.at[kind, head], recv_sem=recvs.at[kind, head],
            device_id=device, device_id_type=MESH,
        )

    def own_to_after(h):
        return remote(kv.at[h, :, rows(4 + core)], kv.at[h, :, rows(2 + core)], 0, h, after)

    def pass_on(h):
        return remote(kv.at[h, :, rows(2 + core)], kv.at[h, :, rows(core)], 1, h, after)

    def share_near(h):
        return remote(kv.at[h, :, rows(2 + core)], kv.at[h, :, rows(2 + core)], 2, h, sibling)

    def share_far(h):
        return remote(kv.at[h, :, rows(core)], kv.at[h, :, rows(core)], 3, h, sibling)

    def output_to_sibling(h):
        return remote(o_buf.at[h, other], o_ref.at[h, core], 4, h, sibling)

    def dquery_to_sibling(h):
        return remote(dq_buf.at[h, other], dq_ref.at[h, core], 5, h, sibling)

    def terms_to_sibling(h):
        return remote(pair_out.at[h], pair_in.at[h], 6, h, sibling)

    def far_terms(h):
        return remote(a_out.at[h], a_in.at[h], 7, h, before)

    def near_terms(h):
        return remote(b_out.at[h], b_in.at[h], 8, h, before)

    def single(src, dst, index):
        return pltpu.make_async_remote_copy(
            src_ref=src, dst_ref=dst, send_sem=one_send.at[index], recv_sem=one_recv.at[index],
            device_id=sibling, device_id_type=MESH,
        )

    own_to_sibling = single(kv.at[:, :, rows(4 + core)], kv.at[:, :, rows(4 + core)], 0)
    query_to_sibling = single(q_ref.at[:, other], q_all.at[:, rows(core)], 1)
    grad_to_sibling = single(g_ref.at[:, other], g_all.at[:, rows(core)], 2)

    query_gain = gain_ref[0:1]
    key_gain = gain_ref[1:2]

    def fill(h, carry):
        kv[h, 0, rows(4 + core)] = normalize(k_ref[h], key_gain)[2]
        kv[h, 1, rows(4 + core)] = v_ref[h]
        return carry

    lax.fori_loop(0, heads, fill, 0)

    barrier = pltpu.get_barrier_semaphore()
    for device in (sibling, after, before):
        pl.semaphore_signal(barrier, inc=1, device_id=device, device_id_type=MESH)
    pl.semaphore_wait(barrier, 3)

    for h in range(AHEAD):
        own_to_after(h).start()
    own_to_sibling.start()
    query_to_sibling.start()
    grad_to_sibling.start()

    part_ref[...] = jnp.zeros_like(part_ref)
    p_bf[...] = jnp.zeros_like(p_bf)
    ds_bf[...] = jnp.zeros_like(ds_bf)
    for h in range(heads):
        q_all[h, rows(core)] = q_ref[h, core]
        g_all[h, rows(core)] = g_ref[h, core]
    for qb in range(2):
        for kb in range(qb, qb + 5):
            behind = (
                (4 + qb - kb) * BLOCK
                + lax.broadcasted_iota(jnp.int32, (BLOCK, BLOCK), 1)
                - lax.broadcasted_iota(jnp.int32, (BLOCK, BLOCK), 0)
            )
            allowed = (
                (behind >= 0)
                & (behind < LOOKBACK_TOKENS)
                & (seg_key[pl.ds(kb * BLOCK, BLOCK)] == seg_query[:, pl.ds(qb * BLOCK, BLOCK)])
            )
            mask[pl.ds(kb * BLOCK, BLOCK), pl.ds(qb * BLOCK, BLOCK)] = jnp.where(
                allowed, 0.0, HIDDEN
            )

    def arrive_near(h):
        own_to_after(h).wait_recv()
        pass_on(h).start()
        share_near(h).start()

    for h in range(AHEAD):
        arrive_near(h)
        own_to_after(h + AHEAD).start()
    own_to_sibling.wait_recv()
    query_to_sibling.wait_recv()
    grad_to_sibling.wait_recv()

    def attend(h):
        query_unit, query_factor, query_normed = normalize(q_all[h], query_gain)
        grad = g_all[h]
        part = jnp.zeros((1, WIDTH), jnp.float32)
        for qb in range(2):
            columns = slice(qb * BLOCK, (qb + 1) * BLOCK)
            top = None
            for i in range(5):
                kb = pl.ds((qb + i) * BLOCK, BLOCK)
                scores = (
                    dot(kv[h, 0, kb], query_normed[columns], NT) * log2_scale + mask[kb, columns]
                )
                s_buf[qb, i] = scores
                tile_top = jnp.max(scores, axis=0, keepdims=True)
                top = tile_top if top is None else jnp.maximum(top, tile_top)
            total = jnp.zeros((1, BLOCK), jnp.float32)
            inner = jnp.zeros((1, BLOCK), jnp.float32)
            for i in range(5):
                kb = pl.ds((qb + i) * BLOCK, BLOCK)
                dprob = dot(kv[h, 1, kb], grad[columns], NT)
                weight = jnp.exp2(s_buf[qb, i] - top)
                s_buf[qb, i] = weight
                d_buf[qb, i] = dprob
                total = total + jnp.sum(weight, axis=0, keepdims=True)
                inner = inner + jnp.sum(weight * dprob, axis=0, keepdims=True)
            inverse = 1.0 / total
            delta = inner * inverse
            for i in range(5):
                kb = pl.ds((qb + i) * BLOCK, BLOCK)
                probs = s_buf[qb, i] * inverse
                p_bf[kb, columns] = probs.astype(jnp.bfloat16)
                ds_bf[kb, columns] = (probs * (d_buf[qb, i] - delta)).astype(jnp.bfloat16)
            window = pl.ds(qb * BLOCK, 5 * BLOCK)
            o_buf[h, qb] = dot(kv[h, 1, window], p_bf[window, columns], TN).T.astype(jnp.bfloat16)
            dquery = dot(kv[h, 0, window], ds_bf[window, columns], TN).T * score_scale
            dq_buf[h, qb], gain_part = norm_backward(
                dquery, query_unit[columns], query_factor[columns], query_gain
            )
            part = part + gain_part
        part_ref[0:1] += part
        for chip in range(3):
            kb = rows(2 * chip + other)
            dkey = dot(ds_bf[kb], query_normed, NN) * score_scale
            pair_out[h, chip, 0] = dkey.astype(jnp.bfloat16)
            pair_out[h, chip, 1] = dot(p_bf[kb], grad, NN).astype(jnp.bfloat16)
        terms_to_sibling(h).start()
        for chip in range(3):
            kb = rows(2 * chip + core)
            held[h, chip, 0] = dot(ds_bf[kb], query_normed, NN) * score_scale
            held[h, chip, 1] = dot(p_bf[kb], grad, NN)
        output_to_sibling(h).start()
        dquery_to_sibling(h).start()
        o_ref[h, core] = o_buf[h, core]
        dq_ref[h, core] = dq_buf[h, core]

    def step(s, carry):
        @pl.when(s < heads)
        def _():
            pass_on(s).wait_recv()
            share_far(s).start()
            share_near(s).wait_recv()
            share_far(s).wait_recv()
            attend(s)

        @pl.when(s + AHEAD < heads)
        def _():
            arrive_near(s + AHEAD)

        @pl.when(s + 2 * AHEAD < heads)
        def _():
            own_to_after(s + 2 * AHEAD).start()

        @pl.when((s >= 1) & (s < heads + 1))
        def _():
            h = s - 1
            terms_to_sibling(h).wait_recv()
            a_out[h] = (held[h, 0] + pair_in[h, 0].astype(jnp.float32)).astype(jnp.bfloat16)
            far_terms(h).start()

        @pl.when((s >= 2) & (s < heads + 2))
        def _():
            h = s - 2
            far_terms(h).wait_recv()
            b_out[h] = (
                held[h, 1] + pair_in[h, 1].astype(jnp.float32) + a_in[h].astype(jnp.float32)
            ).astype(jnp.bfloat16)
            near_terms(h).start()

        @pl.when(s >= 3)
        def _():
            h = s - 3
            near_terms(h).wait_recv()
            term = held[h, 2] + pair_in[h, 2].astype(jnp.float32) + b_in[h].astype(jnp.float32)
            key_unit, key_factor, _ = normalize(k_ref[h], key_gain)
            dk_ref[h], gain_part = norm_backward(term[0], key_unit, key_factor, key_gain)
            dv_ref[h] = term[1].astype(jnp.bfloat16)
            part_ref[1:2] += gain_part

        return carry

    lax.fori_loop(0, heads + 3, step, 0)

    def finish(h, carry):
        output_to_sibling(h).wait_recv()
        dquery_to_sibling(h).wait_recv()
        for copy in (
            own_to_after, pass_on, share_near, share_far, output_to_sibling, dquery_to_sibling,
            terms_to_sibling, far_terms, near_terms,
        ):
            copy(h).wait_send()
        return carry

    lax.fori_loop(0, heads, finish, 0)
    own_to_sibling.wait_send()
    query_to_sibling.wait_send()
    grad_to_sibling.wait_send()


def attention(q, k, v, g, seg_key, seg_query, gains):
    groups = k.shape[0]
    half = jnp.bfloat16
    wide = jnp.float32
    vmem = pl.BlockSpec(memory_space=pltpu.VMEM)
    dma = pltpu.SemaphoreType.DMA
    return pl.pallas_call(
        kernel,
        out_shape=[
            jax.ShapeDtypeStruct((groups, 2, BLOCK, WIDTH), half),
            jax.ShapeDtypeStruct((groups, 2, BLOCK, WIDTH), half),
            jax.ShapeDtypeStruct((groups, BLOCK, WIDTH), half),
            jax.ShapeDtypeStruct((groups, BLOCK, WIDTH), half),
            jax.ShapeDtypeStruct((2, WIDTH), wide),
        ],
        in_specs=[vmem] * 7,
        out_specs=[vmem] * 5,
        scratch_shapes=[
            pltpu.VMEM((groups, 2, SPAN * BLOCK, WIDTH), half),
            pltpu.VMEM((groups, 2 * BLOCK, WIDTH), half),
            pltpu.VMEM((groups, 2 * BLOCK, WIDTH), half),
            pltpu.VMEM((SPAN * BLOCK, 2 * BLOCK), wide),
            pltpu.VMEM((2, 5, BLOCK, BLOCK), wide),
            pltpu.VMEM((2, 5, BLOCK, BLOCK), wide),
            pltpu.VMEM((SPAN * BLOCK, 2 * BLOCK), half),
            pltpu.VMEM((SPAN * BLOCK, 2 * BLOCK), half),
            pltpu.VMEM((groups, 2, BLOCK, WIDTH), half),
            pltpu.VMEM((groups, 2, BLOCK, WIDTH), half),
            pltpu.VMEM((groups, 3, 2, BLOCK, WIDTH), wide),
            pltpu.VMEM((groups, 3, 2, BLOCK, WIDTH), half),
            pltpu.VMEM((groups, 3, 2, BLOCK, WIDTH), half),
            pltpu.VMEM((groups, 2, BLOCK, WIDTH), half),
            pltpu.VMEM((groups, 2, BLOCK, WIDTH), half),
            pltpu.VMEM((groups, 2, BLOCK, WIDTH), half),
            pltpu.VMEM((groups, 2, BLOCK, WIDTH), half),
            dma((3,)),
            dma((3,)),
            dma((9, groups)),
            dma((9, groups)),
        ],
        compiler_params=pltpu.CompilerParams(
            collective_id=0, has_side_effects=True, vmem_limit_bytes=58 * 2**20
        ),
        name="attention",
    )(q, k, v, g, seg_key, seg_query, gains)


def local(queries, keys, values, out_grad, segment_ids, query_gain, key_gain):
    tokens, heads, width = queries.shape[1:]
    groups = keys.shape[2]
    position = lax.axis_index("ctx")
    chip = position // 2
    segments = segment_ids[0]
    padded = jnp.concatenate([jnp.full((4 * tokens,), -1, jnp.int32), segments], axis=0)
    window = lax.dynamic_slice_in_dim(padded, chip * 2 * tokens, SPAN * tokens, 0)
    by_head = lambda array: jnp.swapaxes(array[0], 0, 1)
    pairs = lambda array: by_head(array).reshape(groups, heads // groups, tokens, width)
    output, query_grad, key_grad, value_grad, part = attention(
        pairs(queries), by_head(keys), by_head(values), pairs(out_grad),
        window[:, None], window[None, 4 * tokens :], jnp.stack([query_gain, key_gain]),
    )
    total = lax.psum(part, ("dp", "ctx"))
    by_token = lambda array: jnp.swapaxes(array.reshape(-1, tokens, width), 0, 1)[None]
    return (
        by_token(output), by_token(query_grad), by_token(key_grad), by_token(value_grad),
        total[0], total[1],
    )


def solution(mesh):
    block = P("dp", "ctx", None, None)
    return jax.shard_map(
        local, mesh=mesh,
        in_specs=(block, block, block, block, P("dp", None), P(), P()),
        out_specs=(block, block, block, block, P(), P()),
        check_vma=False,
    )
```

time: 391 us -> 186 us (0.48)
  waiting for transfers between devices: 144 us -> 0 us
  Pallas kernels: 0 us -> 89.7 us
  starting transfers between devices: 71.3 us -> 0 us
  matrix products: 42.3 us -> 0 us
  other arithmetic: 24.6 us -> 1.3 us
  local copies, waits for them, and re-layouts: 23.7 us -> 15.6 us
  blocking collectives: 82.4 us -> 78.1 us
    ppermute x16 -> x0, waiting for transfers between devices: 144 us -> none  [from_behind(): lax.ppermute(value, axis, [(source, source + steps) for source in range(i...]
    pallas_call x0 -> x1, Pallas kernels: none -> 89.7 us  [attention(): pl.pallas_call(kernel, out_shape=[jax.ShapeDtypeStruct((groups, 2, BLOCK,...]
    ppermute x16 -> x0, starting transfers between devices: 71.3 us -> none  [from_behind(): lax.ppermute(value, axis, [(source, source + steps) for source in range(i...]
    dot_general x12 -> x0, matrix products: 42.3 us -> none  [the longest x2 10.3 us: group_block(): jnp.einsum('gqtk,tgqc->kgc', rounded, grad_group, preferred_element_type=...]
    unnamed x69 -> x18, local copies, waits for them, and re-layouts: 19.2 us -> 2.96 us
    reduce_sum x6 -> x0, other arithmetic: 8.53 us -> none  [the longest x2 3.66 us: norm_backward(): jnp.sum(grad * unit, axis=(0, 1))]
    convert_element_type x3 -> x0, other arithmetic: 6.24 us -> none  [the longest x2 3.69 us: normalize(): return (unit, factor, (unit * gain).astype(jnp.bfloat16))]
    transpose x0 -> x3, local copies, waits for them, and re-layouts: none -> 4.95 us  [local(): by_head = lambda array: jnp.swapaxes(array[0], 0, 1)]
  transfers between devices with their start and end apart: 16 -> 0, of which waited for: 7 -> 0; matrix products, arithmetic and copies ran while one was open for 7% -> 0% of each run, Pallas kernels for 0% -> 0%
where the time goes in v1:
time: 186 us; the launch traced here: 185 us
  Pallas kernels  89.7 us (48%)
  blocking collectives  78.1 us (42%)
  local copies, waits for them, and re-layouts  15.6 us (8%)
    pallas_call x1, Pallas kernels, attention(): pl.pallas_call(kernel, out_shape=[jax.ShapeDtypeStruct((groups, 2, BLOCK,...  89.7 us
    psum x1, blocking collectives, local(): total = lax.psum(part, ('dp', 'ctx'))  78.1 us
    transpose x3, local copies, waits for them, and re-layouts, local(): by_head = lambda array: jnp.swapaxes(array[0], 0, 1)  4.95 us
    reshape x2, local copies, waits for them, and re-layouts, local(): array.reshape(-1, tokens, width)  4.61 us

profile of v1, /device:TPU:1, one launch (start us, length us, event | category | flops | bytes accessed | tf_op | source)
XLA Modules:
  0.0 185.5 jit_solution(18338047809995442922)
XLA Ops:
  0.6 0.0 copy-start.6
  0.7 1.3 pad_maximum_fusion.gain_ref
  2.0 1.3 pad_dynamic-slice_fusion
  3.3 0.0 copy-done.6
  3.3 0.1 pad_dynamic-slice_fusion.1
  3.4 1.1 broadcast_in_dim.25.seg_key
  4.5 2.6 %copy.21 = bf16[16,256,128]{2,1,0:T(8,128)(2,1)} copy(bf16[16,256,128]{2,0,1:T(8,128)(2,1)} %bitcast.44) | data formatting | bytes 2097152 | tf_op jit(solution)/shard_map/transpose | solution.py:335
  7.1 0.0 copy-done
  7.1 1.2 copy.24
  8.3 0.0 copy-done.4
  8.3 0.0 copy-done.5
  8.3 1.2 copy_bitcast_fusion.2
  9.5 89.7 %attention.1 = (bf16[8,2,256,128]{3,2,1,0:T(8,128)(2,1)}, bf16[8,2,256,128]{3,2,1,0:T(8,128)(2,1)}, bf16[8,256,128]{2,1,0:T(8,128)(2,1)}, bf16[8,256,128]{2,1,0:T(8,128)(2,1)}, f32[2,128]{1,0:T(2,128)}) custom-call(bf16[8,2,256,128]{3,2,1,0:T(8,128)(2,1)} %bitcast.42, bf16[8,256,128]{2,1,0:T(8,128)(2,1)} %get-tuple-element.31.k_ref, ...), custom_call_target="tpu_custom_call" | custom-call | tf_op jit(solution)/shard_map/attention/pallas_call | solution.py:286
  99.2 0.0 copy-start.1
  99.2 3.0 %copy.35 = bf16[16,256,128]{2,0,1:T(8,128)(2,1)} copy(bf16[16,256,128]{2,1,0:T(8,128)(2,1)} %bitcast.49) | data formatting | bytes 2097152 | tf_op jit(solution)/shard_map/reshape | solution.py:342
  102.2 0.0 copy-done.1
  102.2 1.6 copy.34
  103.9 0.7 copy-done.7
  104.5 78.1 %psum.7 = f32[2,128]{1,0:T(2,128)S(1)} all-reduce(f32[2,128]{1,0:T(2,128)S(1)} %copy-done.7), channel_id=1, replica_groups=mesh['dp'=4,'ctx'=64] {'dp','ctx'}, use_global_device_ids=true, to_apply=%region_0.1 | all-reduce | flops 256 | bytes 2048 | tf_op jit(solution)/shard_map/psum | solution.py:341
  182.7 0.5 slice_bitcast_fusion
  183.2 0.0 copy-done.3
  183.2 1.1 copy.28
  184.3 0.0 copy-done.2
  184.3 1.1 copy.29
  (6 shorter events, 0.0 us)
Async XLA Ops:
  0.6 2.7 %copy-start.6 = (s32[1,16384]{1,0:T(1,128)S(1)}, s32[1,16384]{1,0:T(1,128)}, u32[]{:S(2)}) copy-start(s32[1,16384]{1,0:T(1,128)} %param.11) | copy-start | bytes 196612
  4.5 2.6 %copy-start = (bf16[1,256,16,128]{3,2,1,0:T(8,128)(2,1)S(1)}, bf16[1,256,16,128]{3,2,1,0:T(8,128)(2,1)}, u32[]{:S(2)}) copy-start(bf16[1,256,16,128]{3,2,1,0:T(8,128)(2,1)} %param.10) | copy-start | bytes 3145732
  7.1 1.2 copy-start.4
  7.1 1.2 copy-start.5
  99.2 3.0 %copy-start.1 = (bf16[8,2,256,128]{3,2,1,0:T(8,128)(2,1)S(1)}, bf16[8,2,256,128]{3,2,1,0:T(8,128)(2,1)}, u32[]{:S(2)}) copy-start(bf16[8,2,256,128]{3,2,1,0:T(8,128)(2,1)} %get-tuple-element.12) | copy-start | bytes 3145732
  102.2 81.0 %copy-start.3 = (bf16[8,256,128]{2,1,0:T(8,128)(2,1)S(1)}, bf16[8,256,128]{2,1,0:T(8,128)(2,1)}, u32[]{:S(2)}) copy-start(bf16[8,256,128]{2,1,0:T(8,128)(2,1)} %get-tuple-element.13) | copy-start | bytes 1572868
  103.9 0.7 copy-start.7
  183.2 1.1 copy-start.2

commit v2 on v1

v2 whole, which is shorter than its diff:
```python
import jax
import jax.numpy as jnp
from jax import lax
from jax.experimental import pallas as pl
from jax.experimental.pallas import tpu as pltpu
from jax.sharding import PartitionSpec as P

LOOKBACK_TOKENS = 1024
BLOCK = 256
WIDTH = 128
SPAN = 6
score_scale = 168.0 ** (-0.5)
log2_scale = score_scale * 1.4426950408889634
eps = 1e-06
HIDDEN = -1e30
CHIPS_ALONG_Z = 8
AHEAD = 2

MESH = pl.DeviceIdType.MESH
NT = (((1,), (1,)), ((), ()))
TN = (((0,), (0,)), ((), ()))
NN = (((1,), (0,)), ((), ()))


def dot(a, b, dims):
    return lax.dot_general(a, b, dims, preferred_element_type=jnp.float32)


def rows(block):
    return pl.ds(pl.multiple_of(block * BLOCK, BLOCK), BLOCK)


def normalize(raw, gain):
    wide = raw.astype(jnp.float32)
    factor = lax.rsqrt(jnp.mean(wide * wide, axis=-1, keepdims=True) + eps)
    unit = wide * factor
    return unit, factor, (unit * gain).astype(jnp.bfloat16)


def norm_backward(grad, unit, factor, gain):
    scaled = grad * gain
    inner = jnp.mean(scaled * unit, axis=-1, keepdims=True)
    return (factor * (scaled - unit * inner)).astype(jnp.bfloat16), jnp.sum(
        grad * unit, axis=0, keepdims=True
    )


def kernel(
    q_hbm, k_hbm, v_hbm, g_hbm, seg_ref, gain_q, gain_k,
    o_hbm, dq_hbm, dk_hbm, dv_hbm, total_ref,
    q_in, k_in, v_in, g_in, wide, q_own, g_own,
    kv, q_all, g_all, mask, s_buf, d_buf, p_bf, ds_bf, key_bf, key_unit, o_buf, dq_buf,
    o_in, dq_in, held, pair_out, pair_in, a_out, a_in, b_out, b_in,
    o_wide, dq_wide, dk_wide, dv_wide, part, part_in, z_part, x_part, y_part,
    local_sem, one_send, one_recv, sends, recvs, sum_send, sum_recv,
):
    dp = lax.axis_index("dp")
    me = lax.axis_index("ctx")
    count = lax.axis_size("ctx")
    line = 2 * CHIPS_ALONG_Z
    columns_of_x = count // line
    sequences = lax.axis_size("dp")
    core = lax.rem(me, 2)
    other = 1 - core
    chip = me // 2
    z_at = lax.rem(chip, CHIPS_ALONG_Z)
    x_at = me // line
    sibling = (dp, me + 1 - 2 * core)
    after = (dp, lax.rem(me + 2, count))
    before = (dp, lax.rem(me + count - 2, count))
    heads = kv.shape[0]

    def along_z(d):
        return (dp, x_at * line + 2 * lax.rem(z_at + d, CHIPS_ALONG_Z) + core)

    def along_x(d):
        return (dp, lax.rem(me + d * line, count))

    def along_y(d):
        return (lax.rem(dp + d, sequences), me)

    barrier = pltpu.get_barrier_semaphore()
    friends = [sibling, after, before]
    friends += [along_z(d) for d in range(1, CHIPS_ALONG_Z)]
    friends += [along_x(d) for d in range(1, columns_of_x)]
    friends += [along_y(d) for d in range(1, sequences)]
    for device in friends:
        pl.semaphore_signal(barrier, inc=1, device_id=device, device_id_type=MESH)

    loads = [
        pltpu.make_async_copy(src, dst, local_sem.at[i])
        for i, (src, dst) in enumerate(
            ((k_hbm, k_in), (v_hbm, v_in), (q_hbm, q_in), (g_hbm, g_in))
        )
    ]
    for load in loads:
        load.start()

    def remote(src, dst, kind, head, device):
        return pltpu.make_async_remote_copy(
            src_ref=src, dst_ref=dst, send_sem=sends.at[kind, head], recv_sem=recvs.at[kind, head],
            device_id=device, device_id_type=MESH,
        )

    def own_to_after(h):
        return remote(kv.at[h, :, rows(4 + core)], kv.at[h, :, rows(2 + core)], 0, h, after)

    def pass_on(h):
        return remote(kv.at[h, :, rows(2 + core)], kv.at[h, :, rows(core)], 1, h, after)

    def share_near(h):
        return remote(kv.at[h, :, rows(2 + core)], kv.at[h, :, rows(2 + core)], 2, h, sibling)

    def share_far(h):
        return remote(kv.at[h, :, rows(core)], kv.at[h, :, rows(core)], 3, h, sibling)

    def output_to_sibling(h):
        return remote(o_buf.at[h, other], o_in.at[h], 4, h, sibling)

    def dquery_to_sibling(h):
        return remote(dq_buf.at[h, other], dq_in.at[h], 5, h, sibling)

    def terms_to_sibling(h):
        return remote(pair_out.at[h], pair_in.at[h], 6, h, sibling)

    def far_terms(h):
        return remote(a_out.at[h], a_in.at[h], 7, h, before)

    def near_terms(h):
        return remote(b_out.at[h], b_in.at[h], 8, h, before)

    def single(src, dst, index):
        return pltpu.make_async_remote_copy(
            src_ref=src, dst_ref=dst, send_sem=one_send.at[index], recv_sem=one_recv.at[index],
            device_id=sibling, device_id_type=MESH,
        )

    own_to_sibling = single(kv.at[:, :, rows(4 + core)], kv.at[:, :, rows(4 + core)], 0)
    query_to_sibling = single(q_own.at[:, other], q_all.at[:, rows(core)], 1)
    grad_to_sibling = single(g_own.at[:, other], g_all.at[:, rows(core)], 2)
    part_to_sibling = single(part, part_in, 3)

    def spread(ref, slot, index, device):
        return pltpu.make_async_remote_copy(
            src_ref=ref.at[slot], dst_ref=ref.at[slot],
            send_sem=sum_send.at[index], recv_sem=sum_recv.at[index],
            device_id=device, device_id_type=MESH,
        )

    z_sums = [spread(z_part, z_at, d, along_z(d)) for d in range(1, CHIPS_ALONG_Z)]
    x_sums = [
        spread(x_part, x_at, CHIPS_ALONG_Z + d, along_x(d)) for d in range(1, columns_of_x)
    ]
    y_sums = [
        spread(y_part, dp, CHIPS_ALONG_Z + columns_of_x + d, along_y(d))
        for d in range(1, sequences)
    ]
    query_gain = gain_q[...]
    key_gain = gain_k[...]

    def widen(ref):
        tokens, across, width = ref.shape
        wide[pl.ds(0, tokens * across)] = (
            ref[...].astype(jnp.float32).reshape(tokens * across, width)
        )

    def head_of(h, across):
        return wide[pl.ds(h, BLOCK, stride=across)].astype(jnp.bfloat16)

    loads[0].wait()
    widen(k_in)
    for h in range(heads):
        kv[h, 0, rows(4 + core)] = head_of(h, heads)
    loads[1].wait()
    widen(v_in)
    for h in range(heads):
        kv[h, 1, rows(4 + core)] = head_of(h, heads)

    pl.semaphore_wait(barrier, len(friends))

    for h in range(AHEAD):
        own_to_after(h).start()
    own_to_sibling.start()

    for load, source, own, everything, copy in (
        (loads[2], q_in, q_own, q_all, query_to_sibling),
        (loads[3], g_in, g_own, g_all, grad_to_sibling),
    ):
        load.wait()
        widen(source)
        for h in range(heads):
            for pair in range(2):
                own[h, pair] = head_of(2 * h + pair, 2 * heads)
        copy.start()
        for h in range(heads):
            everything[h, rows(core)] = own[h, core]

    part[...] = jnp.zeros_like(part)
    corner = jnp.zeros((BLOCK, BLOCK), jnp.bfloat16)
    for ref in (p_bf, ds_bf):
        ref[pl.ds(0, BLOCK), pl.ds(BLOCK, BLOCK)] = corner
        ref[pl.ds(5 * BLOCK, BLOCK), pl.ds(0, BLOCK)] = corner

    def arrive_near(h):
        own_to_after(h).wait_recv()
        pass_on(h).start()
        share_near(h).start()

    arrive_near(0)
    own_to_after(AHEAD).start()

    def segments_of(block):
        place = jnp.maximum(2 * chip - 4 + block, 0) * BLOCK
        found = seg_ref[0:1, pl.ds(pl.multiple_of(place, BLOCK), BLOCK)].astype(jnp.float32)
        return jnp.where(2 * chip - 4 + block >= 0, found, -1.0)

    for kb in range(SPAN):
        by_key = jnp.broadcast_to(segments_of(kb), (WIDTH, BLOCK)).T
        for qb in range(2):
            if not qb <= kb < qb + 5:
                continue
            by_query = segments_of(4 + qb)
            for part_at in range(0, BLOCK, WIDTH):
                behind = (
                    (4 + qb - kb) * BLOCK
                    + part_at
                    + lax.broadcasted_iota(jnp.int32, (BLOCK, WIDTH), 1)
                    - lax.broadcasted_iota(jnp.int32, (BLOCK, WIDTH), 0)
                )
                allowed = (
                    (behind >= 0)
                    & (behind < LOOKBACK_TOKENS)
                    & (by_key == by_query[:, part_at : part_at + WIDTH])
                )
                mask[pl.ds(kb * BLOCK, BLOCK), pl.ds(qb * BLOCK + part_at, WIDTH)] = jnp.where(
                    allowed, 0.0, HIDDEN
                )

    for h in range(1, AHEAD):
        arrive_near(h)
        own_to_after(h + AHEAD).start()
    own_to_sibling.wait_recv()
    query_to_sibling.wait_recv()
    grad_to_sibling.wait_recv()

    def attend(h):
        query_unit, query_factor, query_normed = normalize(q_all[h], query_gain)
        key_unit[...], _, key_bf[...] = normalize(kv[h, 0], key_gain)
        grad = g_all[h]
        for qb in range(2):
            columns = slice(qb * BLOCK, (qb + 1) * BLOCK)
            top = None
            for i in range(5):
                kb = pl.ds((qb + i) * BLOCK, BLOCK)
                scores = dot(key_bf[kb], query_normed[columns], NT) * log2_scale + mask[kb, columns]
                s_buf[qb, i] = scores
                tile_top = jnp.max(scores, axis=0, keepdims=True)
                top = tile_top if top is None else jnp.maximum(top, tile_top)
            total = jnp.zeros((1, BLOCK), jnp.float32)
            inner = jnp.zeros((1, BLOCK), jnp.float32)
            for i in range(5):
                kb = pl.ds((qb + i) * BLOCK, BLOCK)
                dprob = dot(kv[h, 1, kb], grad[columns], NT)
                weight = jnp.exp2(s_buf[qb, i] - top)
                s_buf[qb, i] = weight
                d_buf[qb, i] = dprob
                total = total + jnp.sum(weight, axis=0, keepdims=True)
                inner = inner + jnp.sum(weight * dprob, axis=0, keepdims=True)
            inverse = 1.0 / total
            delta = inner * inverse
            for i in range(5):
                kb = pl.ds((qb + i) * BLOCK, BLOCK)
                probs = s_buf[qb, i] * inverse
                p_bf[kb, columns] = probs.astype(jnp.bfloat16)
                ds_bf[kb, columns] = (probs * (d_buf[qb, i] - delta)).astype(jnp.bfloat16)
        key_part = jnp.zeros((1, WIDTH), jnp.float32)
        for near in range(3):
            kb = rows(2 * near + other)
            dkey = dot(ds_bf[kb], query_normed, NN) * score_scale
            pair_out[h, near, 0] = dkey.astype(jnp.bfloat16)
            pair_out[h, near, 1] = dot(p_bf[kb], grad, NN).astype(jnp.bfloat16)
            key_part = key_part + jnp.sum(dkey * key_unit[kb], axis=0, keepdims=True)
        terms_to_sibling(h).start()
        for near in range(3):
            kb = rows(2 * near + core)
            dkey = dot(ds_bf[kb], query_normed, NN) * score_scale
            held[h, near, 0] = dkey
            held[h, near, 1] = dot(p_bf[kb], grad, NN)
            key_part = key_part + jnp.sum(dkey * key_unit[kb], axis=0, keepdims=True)
        query_part = jnp.zeros((1, WIDTH), jnp.float32)
        for qb in range(2):
            columns = slice(qb * BLOCK, (qb + 1) * BLOCK)
            window = pl.ds(qb * BLOCK, 5 * BLOCK)
            dquery = dot(key_bf[window], ds_bf[window, columns], TN).T * score_scale
            dq_buf[h, qb], gain_part = norm_backward(
                dquery, query_unit[columns], query_factor[columns], query_gain
            )
            query_part = query_part + gain_part
            o_buf[h, qb] = dot(kv[h, 1, window], p_bf[window, columns], TN).T.astype(jnp.bfloat16)
        part[0:1] += query_part
        part[1:2] += key_part
        dquery_to_sibling(h).start()
        output_to_sibling(h).start()

    def send_far(h):
        terms_to_sibling(h).wait_recv()
        a_out[h] = (held[h, 0] + pair_in[h, 0].astype(jnp.float32)).astype(jnp.bfloat16)
        far_terms(h).start()

    def send_near(h):
        far_terms(h).wait_recv()
        b_out[h] = (
            held[h, 1] + pair_in[h, 1].astype(jnp.float32) + a_in[h].astype(jnp.float32)
        ).astype(jnp.bfloat16)
        near_terms(h).start()

    def finish_key(h):
        near_terms(h).wait_recv()
        term = held[h, 2] + pair_in[h, 2].astype(jnp.float32) + b_in[h].astype(jnp.float32)
        unit, factor, _ = normalize(kv[h, 0, rows(4 + core)], key_gain)
        grad, _ = norm_backward(term[0], unit, factor, key_gain)
        dk_wide[pl.ds(h, BLOCK, stride=heads)] = grad.astype(jnp.float32)
        dv_wide[pl.ds(h, BLOCK, stride=heads)] = term[1]

    def step(s, carry):
        pass_on(s).wait_recv()
        share_far(s).start()
        share_near(s).wait_recv()
        share_far(s).wait_recv()
        attend(s)

        @pl.when(s + AHEAD < heads)
        def _():
            arrive_near(s + AHEAD)

        @pl.when(s + 2 * AHEAD < heads)
        def _():
            own_to_after(s + 2 * AHEAD).start()

        @pl.when(s >= 1)
        def _():
            send_far(s - 1)

        @pl.when(s >= 2)
        def _():
            send_near(s - 2)

        @pl.when(s >= 3)
        def _():
            finish_key(s - 3)

        return carry

    lax.fori_loop(0, heads, step, 0)

    part_to_sibling.start()
    send_far(heads - 1)
    part_to_sibling.wait_recv()
    z_part[z_at] = part[...] + part_in[...]
    for copy in z_sums:
        copy.start()
    send_near(heads - 2)
    finish_key(heads - 3)

    def natural(into, ours, theirs, h):
        into[pl.ds(2 * h + core, BLOCK, stride=2 * heads)] = ours[h, core].astype(jnp.float32)
        into[pl.ds(2 * h + other, BLOCK, stride=2 * heads)] = theirs[h].astype(jnp.float32)

    def narrow(into, ref):
        tokens, across, width = into.shape
        into[...] = ref[...].reshape(tokens, across, width).astype(jnp.bfloat16)

    for h in range(heads):
        dquery_to_sibling(h).wait_recv()
        output_to_sibling(h).wait_recv()
        natural(dq_wide, dq_buf, dq_in, h)
        natural(o_wide, o_buf, o_in, h)
    send_near(heads - 1)
    for copy in z_sums:
        copy.wait_recv()
    x_part[x_at] = jnp.sum(z_part[...], axis=0)
    for copy in x_sums:
        copy.start()
    finish_key(heads - 2)
    narrow(q_in, dq_wide)
    stores = [pltpu.make_async_copy(q_in, dq_hbm, local_sem.at[0])]
    stores[0].start()
    for copy in x_sums:
        copy.wait_recv()
    y_part[dp] = jnp.sum(x_part[...], axis=0)
    for copy in y_sums:
        copy.start()
    narrow(g_in, o_wide)
    stores.append(pltpu.make_async_copy(g_in, o_hbm, local_sem.at[1]))
    stores[1].start()
    finish_key(heads - 1)
    narrow(k_in, dk_wide)
    stores.append(pltpu.make_async_copy(k_in, dk_hbm, local_sem.at[2]))
    stores[2].start()
    narrow(v_in, dv_wide)
    stores.append(pltpu.make_async_copy(v_in, dv_hbm, local_sem.at[3]))
    stores[3].start()
    for copy in y_sums:
        copy.wait_recv()
    total_ref[...] = jnp.sum(y_part[...], axis=0)

    def sent(h, carry):
        for copy in (
            own_to_after, pass_on, share_near, share_far, output_to_sibling, dquery_to_sibling,
            terms_to_sibling, far_terms, near_terms,
        ):
            copy(h).wait_send()
        return carry

    lax.fori_loop(0, heads, sent, 0)
    for copy in (own_to_sibling, query_to_sibling, grad_to_sibling, part_to_sibling):
        copy.wait_send()
    for copy in z_sums + x_sums + y_sums:
        copy.wait_send()
    for store in stores:
        store.wait()


def attention(q, k, v, g, segments, gain_q, gain_k, sequences, columns_of_x):
    tokens, groups, width = k.shape
    half = jnp.bfloat16
    wide = jnp.float32
    vmem = pl.BlockSpec(memory_space=pltpu.VMEM)
    anywhere = pl.BlockSpec(memory_space=pl.ANY)
    dma = pltpu.SemaphoreType.DMA
    sums = CHIPS_ALONG_Z + columns_of_x + sequences
    return pl.pallas_call(
        kernel,
        out_shape=[
            jax.ShapeDtypeStruct(q.shape, half),
            jax.ShapeDtypeStruct(q.shape, half),
            jax.ShapeDtypeStruct(k.shape, half),
            jax.ShapeDtypeStruct(k.shape, half),
            jax.ShapeDtypeStruct((8, width), wide),
        ],
        in_specs=[anywhere] * 4 + [vmem] * 3,
        out_specs=[anywhere] * 4 + [vmem],
        scratch_shapes=[
            pltpu.VMEM(q.shape, half),
            pltpu.VMEM(k.shape, half),
            pltpu.VMEM(k.shape, half),
            pltpu.VMEM(q.shape, half),
            pltpu.VMEM((2 * groups * tokens, width), wide),
            pltpu.VMEM((groups, 2, tokens, width), half),
            pltpu.VMEM((groups, 2, tokens, width), half),
            pltpu.VMEM((groups, 2, SPAN * tokens, width), half),
            pltpu.VMEM((groups, 2 * tokens, width), half),
            pltpu.VMEM((groups, 2 * tokens, width), half),
            pltpu.VMEM((SPAN * tokens, 2 * tokens), wide),
            pltpu.VMEM((2, 5, tokens, tokens), wide),
            pltpu.VMEM((2, 5, tokens, tokens), wide),
            pltpu.VMEM((SPAN * tokens, 2 * tokens), half),
            pltpu.VMEM((SPAN * tokens, 2 * tokens), half),
            pltpu.VMEM((SPAN * tokens, width), half),
            pltpu.VMEM((SPAN * tokens, width), wide),
            pltpu.VMEM((groups, 2, tokens, width), half),
            pltpu.VMEM((groups, 2, tokens, width), half),
            pltpu.VMEM((groups, tokens, width), half),
            pltpu.VMEM((groups, tokens, width), half),
            pltpu.VMEM((groups, 3, 2, tokens, width), wide),
            pltpu.VMEM((groups, 3, 2, tokens, width), half),
            pltpu.VMEM((groups, 3, 2, tokens, width), half),
            pltpu.VMEM((groups, 2, tokens, width), half),
            pltpu.VMEM((groups, 2, tokens, width), half),
            pltpu.VMEM((groups, 2, tokens, width), half),
            pltpu.VMEM((groups, 2, tokens, width), half),
            pltpu.VMEM((2 * groups * tokens, width), wide),
            pltpu.VMEM((2 * groups * tokens, width), wide),
            pltpu.VMEM((groups * tokens, width), wide),
            pltpu.VMEM((groups * tokens, width), wide),
            pltpu.VMEM((8, width), wide),
            pltpu.VMEM((8, width), wide),
            pltpu.VMEM((CHIPS_ALONG_Z, 8, width), wide),
            pltpu.VMEM((columns_of_x, 8, width), wide),
            pltpu.VMEM((sequences, 8, width), wide),
            dma((4,)),
            dma((4,)),
            dma((4,)),
            dma((9, groups)),
            dma((9, groups)),
            dma((sums,)),
            dma((sums,)),
        ],
        compiler_params=pltpu.CompilerParams(
            collective_id=0, has_side_effects=True, vmem_limit_bytes=60 * 2**20
        ),
        name="attention",
    )(q, k, v, g, segments, gain_q, gain_k)


def local(queries, keys, values, out_grad, segment_ids, query_gain, key_gain):
    sequences = lax.axis_size("dp")
    columns_of_x = lax.axis_size("ctx") // (2 * CHIPS_ALONG_Z)
    output, query_grad, key_grad, value_grad, total = attention(
        queries[0], keys[0], values[0], out_grad[0], segment_ids,
        query_gain[None], key_gain[None], sequences, columns_of_x,
    )
    return (
        output[None], query_grad[None], key_grad[None], value_grad[None], total[0], total[1],
    )


def solution(mesh):
    block = P("dp", "ctx", None, None)
    return jax.shard_map(
        local, mesh=mesh,
        in_specs=(block, block, block, block, P("dp", None), P(), P()),
        out_specs=(block, block, block, block, P(), P()),
        check_vma=False,
    )
```

time: 186 us -> 99.1 us (0.53)
  blocking collectives: 78.1 us -> 0 us
  local copies, waits for them, and re-layouts: 15.6 us -> 7.14 us
    psum x1 -> x0, blocking collectives: 78.1 us -> none  [local(): total = lax.psum(part, ('dp', 'ctx'))]
    transpose x3 -> x0, local copies, waits for them, and re-layouts: 4.95 us -> none  [local(): by_head = lambda array: jnp.swapaxes(array[0], 0, 1)]
    reshape x2 -> x0, local copies, waits for them, and re-layouts: 4.61 us -> none  [local(): array.reshape(-1, tokens, width)]
    unnamed x18 -> x10, local copies, waits for them, and re-layouts: 2.96 us -> 5.88 us
where the time goes in v2:
time: 99.1 us; the launch traced here: 97.3 us
  Pallas kernels  89.5 us (90%)
  local copies, waits for them, and re-layouts  7.14 us (7%)
    pallas_call x1, Pallas kernels, attention(): pl.pallas_call(kernel, out_shape=[jax.ShapeDtypeStruct(q.shape, half), ja...  89.5 us
    unnamed x10, local copies, waits for them, and re-layouts  5.88 us

profile of v2, /device:TPU:1, one launch (start us, length us, event | category | flops | bytes accessed | tf_op | source)
XLA Modules:
  0.0 97.3 jit_solution(15277238832662732687)
XLA Ops:
  0.6 89.5 %attention.1 = (bf16[256,16,128]{2,1,0:T(8,128)(2,1)}, bf16[256,16,128]{2,1,0:T(8,128)(2,1)}, bf16[256,8,128]{2,1,0:T(8,128)(2,1)}, bf16[256,8,128]{2,1,0:T(8,128)(2,1)}, f32[8,128]{1,0:T(8,128)}) custom-call(bf16[256,16,128]{2,1,0:T(8,128)(2,1)} %bitcast.14, bf16[256,8,128]{2,1,0:T(8,128)(2,1)} %bitcast.20, bf16[256,8,128]{2,1,0:T(8,128)(2,1)} %bitcast.21, ...), custom_call_target="tpu_custom_call" | custom-call | tf_op jit(solution)/shard_map/attention/pallas_call | solution.py:432
  90.1 1.3 %slice_bitcast_fusion = (f32[128]{0:T(128)}, f32[128]{0:T(128)}) fusion(f32[8,128]{1,0:T(8,128)} %get-tuple-element.15), kind=kLoop, calls=%fused_computation | loop fusion | bytes 2048 | tf_op jit(solution)/shard_map/squeeze | solution.py:504
  91.4 0.0 copy-start
  91.4 2.5 %copy.17 = bf16[1,256,16,128]{3,2,1,0:T(8,128)(2,1)} copy(bf16[1,256,16,128]{3,2,1,0:T(8,128)(2,1)} %bitcast.17) | data formatting | bytes 2097152
  93.8 0.0 copy-done
  93.8 0.0 copy-start.2
  93.8 1.0 copy.18
  94.8 0.4 copy-done.2
  95.2 0.0 copy-start.1
  95.2 0.8 copy.19
  96.0 0.4 copy-done.1
  96.5 0.8 copy.20
Async XLA Ops:
  91.4 2.5 %copy-start = (bf16[256,16,128]{2,1,0:T(8,128)(2,1)S(1)}, bf16[256,16,128]{2,1,0:T(8,128)(2,1)}, u32[]{:S(2)}) copy-start(bf16[256,16,128]{2,1,0:T(8,128)(2,1)} %get-tuple-element.12) | copy-start | bytes 3145732
  93.8 1.4 %copy-start.2 = (bf16[256,8,128]{2,1,0:T(8,128)(2,1)S(1)}, bf16[256,8,128]{2,1,0:T(8,128)(2,1)}, u32[]{:S(2)}) copy-start(bf16[256,8,128]{2,1,0:T(8,128)(2,1)} %get-tuple-element.13) | copy-start | bytes 1572868
  95.2 1.2 %copy-start.1 = (bf16[256,8,128]{2,1,0:T(8,128)(2,1)S(1)}, bf16[256,8,128]{2,1,0:T(8,128)(2,1)}, u32[]{:S(2)}) copy-start(bf16[256,8,128]{2,1,0:T(8,128)(2,1)} %get-tuple-element.14) | copy-start | bytes 1572868

commit v3 on v2

--- a/solution.py
+++ b/solution.py
@@ -49,7 +49,7 @@
     q_hbm, k_hbm, v_hbm, g_hbm, seg_ref, gain_q, gain_k,
     o_hbm, dq_hbm, dk_hbm, dv_hbm, total_ref,
     q_in, k_in, v_in, g_in, wide, q_own, g_own,
-    kv, q_all, g_all, mask, s_buf, d_buf, p_bf, ds_bf, key_bf, key_unit, o_buf, dq_buf,
+    kv, q_all, g_all, mask, s_buf, d_buf, p_bf, ds_bf, key_own, o_buf, dq_buf,
     o_in, dq_in, held, pair_out, pair_in, a_out, a_in, b_out, b_in,
     o_wide, dq_wide, dk_wide, dv_wide, part, part_in, z_part, x_part, y_part,
     local_sem, one_send, one_recv, sends, recvs, sum_send, sum_recv,
@@ -170,7 +170,8 @@
     loads[0].wait()
     widen(k_in)
     for h in range(heads):
-        kv[h, 0, rows(4 + core)] = head_of(h, heads)
+        key_own[h] = head_of(h, heads)
+        kv[h, 0, rows(4 + core)] = normalize(key_own[h], key_gain)[2]
     loads[1].wait()
     widen(v_in)
     for h in range(heads):
@@ -245,14 +246,13 @@
 
     def attend(h):
         query_unit, query_factor, query_normed = normalize(q_all[h], query_gain)
-        key_unit[...], _, key_bf[...] = normalize(kv[h, 0], key_gain)
         grad = g_all[h]
         for qb in range(2):
             columns = slice(qb * BLOCK, (qb + 1) * BLOCK)
             top = None
             for i in range(5):
                 kb = pl.ds((qb + i) * BLOCK, BLOCK)
-                scores = dot(key_bf[kb], query_normed[columns], NT) * log2_scale + mask[kb, columns]
+                scores = dot(kv[h, 0, kb], query_normed[columns], NT) * log2_scale + mask[kb, columns]
                 s_buf[qb, i] = scores
                 tile_top = jnp.max(scores, axis=0, keepdims=True)
                 top = tile_top if top is None else jnp.maximum(top, tile_top)
@@ -279,26 +279,30 @@
             dkey = dot(ds_bf[kb], query_normed, NN) * score_scale
             pair_out[h, near, 0] = dkey.astype(jnp.bfloat16)
             pair_out[h, near, 1] = dot(p_bf[kb], grad, NN).astype(jnp.bfloat16)
-            key_part = key_part + jnp.sum(dkey * key_unit[kb], axis=0, keepdims=True)
+            key_part = key_part + jnp.sum(
+                dkey * kv[h, 0, kb].astype(jnp.float32), axis=0, keepdims=True
+            )
         terms_to_sibling(h).start()
         for near in range(3):
             kb = rows(2 * near + core)
             dkey = dot(ds_bf[kb], query_normed, NN) * score_scale
             held[h, near, 0] = dkey
             held[h, near, 1] = dot(p_bf[kb], grad, NN)
-            key_part = key_part + jnp.sum(dkey * key_unit[kb], axis=0, keepdims=True)
+            key_part = key_part + jnp.sum(
+                dkey * kv[h, 0, kb].astype(jnp.float32), axis=0, keepdims=True
+            )
         query_part = jnp.zeros((1, WIDTH), jnp.float32)
         for qb in range(2):
             columns = slice(qb * BLOCK, (qb + 1) * BLOCK)
             window = pl.ds(qb * BLOCK, 5 * BLOCK)
-            dquery = dot(key_bf[window], ds_bf[window, columns], TN).T * score_scale
+            dquery = dot(kv[h, 0, window], ds_bf[window, columns], TN).T * score_scale
             dq_buf[h, qb], gain_part = norm_backward(
                 dquery, query_unit[columns], query_factor[columns], query_gain
             )
             query_part = query_part + gain_part
             o_buf[h, qb] = dot(kv[h, 1, window], p_bf[window, columns], TN).T.astype(jnp.bfloat16)
         part[0:1] += query_part
-        part[1:2] += key_part
+        part[1:2] += key_part / key_gain
         dquery_to_sibling(h).start()
         output_to_sibling(h).start()
 
@@ -317,18 +321,24 @@
     def finish_key(h):
         near_terms(h).wait_recv()
         term = held[h, 2] + pair_in[h, 2].astype(jnp.float32) + b_in[h].astype(jnp.float32)
-        unit, factor, _ = normalize(kv[h, 0, rows(4 + core)], key_gain)
+        unit, factor, _ = normalize(key_own[h], key_gain)
         grad, _ = norm_backward(term[0], unit, factor, key_gain)
         dk_wide[pl.ds(h, BLOCK, stride=heads)] = grad.astype(jnp.float32)
         dv_wide[pl.ds(h, BLOCK, stride=heads)] = term[1]
 
     def step(s, carry):
-        pass_on(s).wait_recv()
-        share_far(s).start()
         share_near(s).wait_recv()
         share_far(s).wait_recv()
         attend(s)
 
+        @pl.when(s == heads - 1)
+        def _():
+            x_part[x_at] = part[...]
+            for copy in x_sums:
+                copy.start()
+
+        send_far(s)
+
         @pl.when(s + AHEAD < heads)
         def _():
             arrive_near(s + AHEAD)
@@ -337,30 +347,24 @@
         def _():
             own_to_after(s + 2 * AHEAD).start()
 
+        @pl.when(s + 1 < heads)
+        def _():
+            pass_on(s + 1).wait_recv()
+            share_far(s + 1).start()
+
         @pl.when(s >= 1)
         def _():
-            send_far(s - 1)
+            send_near(s - 1)
 
         @pl.when(s >= 2)
         def _():
-            send_near(s - 2)
-
-        @pl.when(s >= 3)
-        def _():
-            finish_key(s - 3)
+            finish_key(s - 2)
 
         return carry
 
+    pass_on(0).wait_recv()
+    share_far(0).start()
     lax.fori_loop(0, heads, step, 0)
-
-    part_to_sibling.start()
-    send_far(heads - 1)
-    part_to_sibling.wait_recv()
-    z_part[z_at] = part[...] + part_in[...]
-    for copy in z_sums:
-        copy.start()
-    send_near(heads - 2)
-    finish_key(heads - 3)
 
     def natural(into, ours, theirs, h):
         into[pl.ds(2 * h + core, BLOCK, stride=2 * heads)] = ours[h, core].astype(jnp.float32)
@@ -370,29 +374,36 @@
         tokens, across, width = into.shape
         into[...] = ref[...].reshape(tokens, across, width).astype(jnp.bfloat16)
 
-    for h in range(heads):
-        dquery_to_sibling(h).wait_recv()
-        output_to_sibling(h).wait_recv()
-        natural(dq_wide, dq_buf, dq_in, h)
-        natural(o_wide, o_buf, o_in, h)
-    send_near(heads - 1)
-    for copy in z_sums:
-        copy.wait_recv()
-    x_part[x_at] = jnp.sum(z_part[...], axis=0)
-    for copy in x_sums:
-        copy.start()
-    finish_key(heads - 2)
-    narrow(q_in, dq_wide)
-    stores = [pltpu.make_async_copy(q_in, dq_hbm, local_sem.at[0])]
-    stores[0].start()
     for copy in x_sums:
         copy.wait_recv()
     y_part[dp] = jnp.sum(x_part[...], axis=0)
     for copy in y_sums:
         copy.start()
+    for h in range(heads):
+        dquery_to_sibling(h).wait_recv()
+        natural(dq_wide, dq_buf, dq_in, h)
+    for copy in y_sums:
+        copy.wait_recv()
+    part[...] = jnp.sum(y_part[...], axis=0)
+    part_to_sibling.start()
+    narrow(q_in, dq_wide)
+    stores = [pltpu.make_async_copy(q_in, dq_hbm, local_sem.at[0])]
+    stores[0].start()
+    part_to_sibling.wait_recv()
+    z_part[z_at] = part[...] + part_in[...]
+    for copy in z_sums:
+        copy.start()
+    send_near(heads - 1)
+    for h in range(heads):
+        output_to_sibling(h).wait_recv()
+        natural(o_wide, o_buf, o_in, h)
     narrow(g_in, o_wide)
     stores.append(pltpu.make_async_copy(g_in, o_hbm, local_sem.at[1]))
     stores[1].start()
+    finish_key(heads - 2)
+    for copy in z_sums:
+        copy.wait_recv()
+    total_ref[...] = jnp.sum(z_part[...], axis=0)
     finish_key(heads - 1)
     narrow(k_in, dk_wide)
     stores.append(pltpu.make_async_copy(k_in, dk_hbm, local_sem.at[2]))
@@ -400,9 +411,6 @@
     narrow(v_in, dv_wide)
     stores.append(pltpu.make_async_copy(v_in, dv_hbm, local_sem.at[3]))
     stores[3].start()
-    for copy in y_sums:
-        copy.wait_recv()
-    total_ref[...] = jnp.sum(y_part[...], axis=0)
 
     def sent(h, carry):
         for copy in (
@@ -456,8 +464,7 @@
             pltpu.VMEM((2, 5, tokens, tokens), wide),
             pltpu.VMEM((SPAN * tokens, 2 * tokens), half),
             pltpu.VMEM((SPAN * tokens, 2 * tokens), half),
-            pltpu.VMEM((SPAN * tokens, width), half),
-            pltpu.VMEM((SPAN * tokens, width), wide),
+            pltpu.VMEM((groups, tokens, width), half),
             pltpu.VMEM((groups, 2, tokens, width), half),
             pltpu.VMEM((groups, 2, tokens, width), half),
             pltpu.VMEM((groups, tokens, width), half),
@@ -493,15 +500,60 @@
     )(q, k, v, g, segments, gain_q, gain_k)
 
 
+def deliver_kernel(
+    o, dq, dk, dv, total, o_out, dq_out, dk_out, dv_out, gain_q, gain_k,
+    o_held, dq_held, dk_held, dv_held, load_sem, store_sem,
+):
+    loads = []
+    stores = []
+    for src, held, dst, pieces in (
+        (o, o_held, o_out, 4), (dq, dq_held, dq_out, 4),
+        (dk, dk_held, dk_out, 2), (dv, dv_held, dv_out, 2),
+    ):
+        size = src.shape[0] // pieces
+        for piece in range(pieces):
+            span = pl.ds(piece * size, size)
+            at = len(loads)
+            loads.append(pltpu.make_async_copy(src.at[span], held.at[span], load_sem.at[at]))
+            stores.append(pltpu.make_async_copy(held.at[span], dst.at[span], store_sem.at[at]))
+    for load in loads:
+        load.start()
+    gain_q[...] = total[0:1]
+    gain_k[...] = total[1:2]
+    for load, store in zip(loads, stores):
+        load.wait()
+        store.start()
+    for store in stores:
+        store.wait()
+
+
+def deliver(output, query_grad, key_grad, value_grad, total):
+    vmem = pl.BlockSpec(memory_space=pltpu.VMEM)
+    anywhere = pl.BlockSpec(memory_space=pl.ANY)
+    arrays = (output, query_grad, key_grad, value_grad)
+    gain = jax.ShapeDtypeStruct((1, total.shape[1]), total.dtype)
+    return pl.pallas_call(
+        deliver_kernel,
+        out_shape=[jax.ShapeDtypeStruct(array.shape, array.dtype) for array in arrays] + [gain] * 2,
+        in_specs=[anywhere] * 4 + [vmem],
+        out_specs=[anywhere] * 4 + [vmem] * 2,
+        scratch_shapes=[pltpu.VMEM(array.shape, array.dtype) for array in arrays]
+        + [pltpu.SemaphoreType.DMA((12,))] * 2,
+        name="deliver",
+    )(*arrays, total)
+
+
 def local(queries, keys, values, out_grad, segment_ids, query_gain, key_gain):
     sequences = lax.axis_size("dp")
     columns_of_x = lax.axis_size("ctx") // (2 * CHIPS_ALONG_Z)
-    output, query_grad, key_grad, value_grad, total = attention(
+    results = attention(
         queries[0], keys[0], values[0], out_grad[0], segment_ids,
         query_gain[None], key_gain[None], sequences, columns_of_x,
     )
+    output, query_grad, key_grad, value_grad, query_total, key_total = deliver(*results)
     return (
-        output[None], query_grad[None], key_grad[None], value_grad[None], total[0], total[1],
+        output[None], query_grad[None], key_grad[None], value_grad[None],
+        query_total[0], key_total[0],
     )
 
 

time: 99.1 us -> 92.9 us (0.937)
  local copies, waits for them, and re-layouts: 7.14 us -> 0 us
  Pallas kernels: 89.5 us -> 90.8 us
    unnamed x10 -> x0, local copies, waits for them, and re-layouts: 5.88 us -> none
    pallas_call x0 -> x1, Pallas kernels: none -> 4.01 us  [deliver(): pl.pallas_call(deliver_kernel, out_shape=[jax.ShapeDtypeStruct(array.shap...]
    pallas_call x1, Pallas kernels: 89.5 us -> 86.8 us  [attention(): pl.pallas_call(kernel, out_shape=[jax.ShapeDtypeStruct(q.shape, half), ja...]
    squeeze x1 -> x0, local copies, waits for them, and re-layouts: 1.25 us -> none  [local(): total[1]]
where the time goes in v3:
time: 92.9 us; the launch traced here: 91.5 us
  Pallas kernels  90.8 us (98%)
    pallas_call x1, Pallas kernels, attention(): pl.pallas_call(kernel, out_shape=[jax.ShapeDtypeStruct(q.shape, half), ja...  86.8 us
    pallas_call x1, Pallas kernels, deliver(): pl.pallas_call(deliver_kernel, out_shape=[jax.ShapeDtypeStruct(array.shap...  4.01 us

profile of v3, /device:TPU:1, one launch (start us, length us, event | category | flops | bytes accessed | tf_op | source)
XLA Modules:
  0.0 91.5 jit_solution(14655144813961978309)
XLA Ops:
  0.6 86.8 %attention.1 = (bf16[256,16,128]{2,1,0:T(8,128)(2,1)}, bf16[256,16,128]{2,1,0:T(8,128)(2,1)}, bf16[256,8,128]{2,1,0:T(8,128)(2,1)}, bf16[256,8,128]{2,1,0:T(8,128)(2,1)}, f32[8,128]{1,0:T(8,128)}) custom-call(bf16[256,16,128]{2,1,0:T(8,128)(2,1)} %bitcast.12, bf16[256,8,128]{2,1,0:T(8,128)(2,1)} %bitcast.14, bf16[256,8,128]{2,1,0:T(8,128)(2,1)} %bitcast.15, ...), custom_call_target="tpu_custom_call" | custom-call | tf_op jit(solution)/shard_map/attention/pallas_call | solution.py:440
  87.5 4.0 %deliver.1 = (bf16[256,16,128]{2,1,0:T(8,128)(2,1)}, bf16[256,16,128]{2,1,0:T(8,128)(2,1)}, bf16[256,8,128]{2,1,0:T(8,128)(2,1)}, bf16[256,8,128]{2,1,0:T(8,128)...) custom-call(bf16[256,16,128]{2,1,0:T(8,128)(2,1)} %get-tuple-element.17.o, bf16[256,16,128]{2,1,0:T(8,128)(2,1)} %get-tuple-element.18.dq, ...), custom_call_target="tpu_custom_call" | custom-call | tf_op jit(solution)/shard_map/deliver/pallas_call | solution.py:535

commit v4 on v3

--- a/solution.py
+++ b/solution.py
@@ -69,6 +69,11 @@
     after = (dp, lax.rem(me + 2, count))
     before = (dp, lax.rem(me + count - 2, count))
     heads = kv.shape[0]
+    first = jnp.where(chip == 0, 1, 0)
+    last = jnp.where(chip == count // 2 - 1, 1, 0)
+
+    def unless(flag, act):
+        pl.when(flag == 0)(act)
 
     def along_z(d):
         return (dp, x_at * line + 2 * lax.rem(z_at + d, CHIPS_ALONG_Z) + core)
@@ -80,12 +85,20 @@
         return (lax.rem(dp + d, sequences), me)
 
     barrier = pltpu.get_barrier_semaphore()
-    friends = [sibling, after, before]
+    friends = [sibling]
     friends += [along_z(d) for d in range(1, CHIPS_ALONG_Z)]
     friends += [along_x(d) for d in range(1, columns_of_x)]
     friends += [along_y(d) for d in range(1, sequences)]
     for device in friends:
         pl.semaphore_signal(barrier, inc=1, device_id=device, device_id_type=MESH)
+
+    @pl.when(last == 0)
+    def _():
+        pl.semaphore_signal(barrier, inc=1, device_id=after, device_id_type=MESH)
+
+    @pl.when(first == 0)
+    def _():
+        pl.semaphore_signal(barrier, inc=1, device_id=before, device_id_type=MESH)
 
     loads = [
         pltpu.make_async_copy(src, dst, local_sem.at[i])
@@ -123,11 +136,11 @@
     def terms_to_sibling(h):
         return remote(pair_out.at[h], pair_in.at[h], 6, h, sibling)
 
-    def far_terms(h):
-        return remote(a_out.at[h], a_in.at[h], 7, h, before)
-
-    def near_terms(h):
-        return remote(b_out.at[h], b_in.at[h], 8, h, before)
+    def far_terms(h, side):
+        return remote(a_out.at[h, side], a_in.at[h, side], 7 + side, h, before)
+
+    def near_terms(h, side):
+        return remote(b_out.at[h, side], b_in.at[h, side], 9 + side, h, before)
 
     def single(src, dst, index):
         return pltpu.make_async_remote_copy(
@@ -177,10 +190,10 @@
     for h in range(heads):
         kv[h, 1, rows(4 + core)] = head_of(h, heads)
 
-    pl.semaphore_wait(barrier, len(friends))
+    pl.semaphore_wait(barrier, len(friends) + 2 - first - last)
 
     for h in range(AHEAD):
-        own_to_after(h).start()
+        unless(last, own_to_after(h).start)
     own_to_sibling.start()
 
     for load, source, own, everything, copy in (
@@ -197,18 +210,31 @@
             everything[h, rows(core)] = own[h, core]
 
     part[...] = jnp.zeros_like(part)
+
+    @pl.when(first == 1)
+    def _():
+        nothing = jnp.zeros((2, BLOCK, WIDTH), jnp.bfloat16)
+        for h in range(heads):
+            kv[h, :, rows(core)] = nothing
+            kv[h, :, rows(2 + core)] = nothing
+
+    @pl.when(last == 1)
+    def _():
+        a_in[...] = jnp.zeros_like(a_in)
+        b_in[...] = jnp.zeros_like(b_in)
+
     corner = jnp.zeros((BLOCK, BLOCK), jnp.bfloat16)
     for ref in (p_bf, ds_bf):
         ref[pl.ds(0, BLOCK), pl.ds(BLOCK, BLOCK)] = corner
         ref[pl.ds(5 * BLOCK, BLOCK), pl.ds(0, BLOCK)] = corner
 
     def arrive_near(h):
-        own_to_after(h).wait_recv()
-        pass_on(h).start()
+        unless(first, own_to_after(h).wait_recv)
+        unless(last, pass_on(h).start)
         share_near(h).start()
 
     arrive_near(0)
-    own_to_after(AHEAD).start()
+    unless(last, own_to_after(AHEAD).start)
 
     def segments_of(block):
         place = jnp.maximum(2 * chip - 4 + block, 0) * BLOCK
@@ -239,7 +265,7 @@
 
     for h in range(1, AHEAD):
         arrive_near(h)
-        own_to_after(h + AHEAD).start()
+        unless(last, own_to_after(h + AHEAD).start)
     own_to_sibling.wait_recv()
     query_to_sibling.wait_recv()
     grad_to_sibling.wait_recv()
@@ -308,23 +334,35 @@
 
     def send_far(h):
         terms_to_sibling(h).wait_recv()
-        a_out[h] = (held[h, 0] + pair_in[h, 0].astype(jnp.float32)).astype(jnp.bfloat16)
-        far_terms(h).start()
+        for side in range(2):
+            a_out[h, side] = (
+                held[h, 0, side] + pair_in[h, 0, side].astype(jnp.float32)
+            ).astype(jnp.bfloat16)
+            unless(first, far_terms(h, side).start)
 
     def send_near(h):
-        far_terms(h).wait_recv()
-        b_out[h] = (
-            held[h, 1] + pair_in[h, 1].astype(jnp.float32) + a_in[h].astype(jnp.float32)
-        ).astype(jnp.bfloat16)
-        near_terms(h).start()
+        for side in range(2):
+            unless(last, far_terms(h, side).wait_recv)
+            b_out[h, side] = (
+                held[h, 1, side]
+                + pair_in[h, 1, side].astype(jnp.float32)
+                + a_in[h, side].astype(jnp.float32)
+            ).astype(jnp.bfloat16)
+            unless(first, near_terms(h, side).start)
 
     def finish_key(h):
-        near_terms(h).wait_recv()
-        term = held[h, 2] + pair_in[h, 2].astype(jnp.float32) + b_in[h].astype(jnp.float32)
+        terms = []
+        for side in range(2):
+            unless(last, near_terms(h, side).wait_recv)
+            terms.append(
+                held[h, 2, side]
+                + pair_in[h, 2, side].astype(jnp.float32)
+                + b_in[h, side].astype(jnp.float32)
+            )
         unit, factor, _ = normalize(key_own[h], key_gain)
-        grad, _ = norm_backward(term[0], unit, factor, key_gain)
+        grad, _ = norm_backward(terms[0], unit, factor, key_gain)
         dk_wide[pl.ds(h, BLOCK, stride=heads)] = grad.astype(jnp.float32)
-        dv_wide[pl.ds(h, BLOCK, stride=heads)] = term[1]
+        dv_wide[pl.ds(h, BLOCK, stride=heads)] = terms[1]
 
     def step(s, carry):
         share_near(s).wait_recv()
@@ -343,13 +381,13 @@
         def _():
             arrive_near(s + AHEAD)
 
-        @pl.when(s + 2 * AHEAD < heads)
+        @pl.when((s + 2 * AHEAD < heads) & (last == 0))
         def _():
             own_to_after(s + 2 * AHEAD).start()
 
         @pl.when(s + 1 < heads)
         def _():
-            pass_on(s + 1).wait_recv()
+            unless(first, pass_on(s + 1).wait_recv)
             share_far(s + 1).start()
 
         @pl.when(s >= 1)
@@ -362,7 +400,7 @@
 
         return carry
 
-    pass_on(0).wait_recv()
+    unless(first, pass_on(0).wait_recv)
     share_far(0).start()
     lax.fori_loop(0, heads, step, 0)
 
@@ -401,9 +439,6 @@
     stores.append(pltpu.make_async_copy(g_in, o_hbm, local_sem.at[1]))
     stores[1].start()
     finish_key(heads - 2)
-    for copy in z_sums:
-        copy.wait_recv()
-    total_ref[...] = jnp.sum(z_part[...], axis=0)
     finish_key(heads - 1)
     narrow(k_in, dk_wide)
     stores.append(pltpu.make_async_copy(k_in, dk_hbm, local_sem.at[2]))
@@ -411,13 +446,20 @@
     narrow(v_in, dv_wide)
     stores.append(pltpu.make_async_copy(v_in, dv_hbm, local_sem.at[3]))
     stores[3].start()
+    for copy in z_sums:
+        copy.wait_recv()
+    total_ref[...] = jnp.sum(z_part[...], axis=0)
 
     def sent(h, carry):
         for copy in (
-            own_to_after, pass_on, share_near, share_far, output_to_sibling, dquery_to_sibling,
-            terms_to_sibling, far_terms, near_terms,
+            share_near, share_far, output_to_sibling, dquery_to_sibling, terms_to_sibling,
         ):
             copy(h).wait_send()
+        for copy in (own_to_after(h), pass_on(h)):
+            unless(last, copy.wait_send)
+        for side in range(2):
+            unless(first, far_terms(h, side).wait_send)
+            unless(first, near_terms(h, side).wait_send)
         return carry
 
     lax.fori_loop(0, heads, sent, 0)
@@ -488,8 +530,8 @@
             dma((4,)),
             dma((4,)),
             dma((4,)),
-            dma((9, groups)),
-            dma((9, groups)),
+            dma((11, groups)),
+            dma((11, groups)),
             dma((sums,)),
             dma((sums,)),
         ],

time: 92.9 us -> 92 us (level); the launches traced: 91.5 us -> 91.9 us
  no operation moved by 1% of the time
where the time goes in v4:
time: 92 us; the launch traced here: 91.9 us
  Pallas kernels  91.2 us (99%)
    pallas_call x1, Pallas kernels, attention(): pl.pallas_call(kernel, out_shape=[jax.ShapeDtypeStruct(q.shape, half), ja...  87.2 us
    pallas_call x1, Pallas kernels, deliver(): pl.pallas_call(deliver_kernel, out_shape=[jax.ShapeDtypeStruct(array.shap...  4.01 us

profile of v4, /device:TPU:1, one launch (start us, length us, event | category | flops | bytes accessed | tf_op | source)
XLA Modules:
  0.0 91.9 jit_solution(9229298097607542427)
XLA Ops:
  0.6 87.2 %attention.1 = (bf16[256,16,128]{2,1,0:T(8,128)(2,1)}, bf16[256,16,128]{2,1,0:T(8,128)(2,1)}, bf16[256,8,128]{2,1,0:T(8,128)(2,1)}, bf16[256,8,128]{2,1,0:T(8,128)(2,1)}, f32[8,128]{1,0:T(8,128)}) custom-call(bf16[256,16,128]{2,1,0:T(8,128)(2,1)} %bitcast.12, bf16[256,8,128]{2,1,0:T(8,128)(2,1)} %bitcast.14, bf16[256,8,128]{2,1,0:T(8,128)(2,1)} %bitcast.15, ...), custom_call_target="tpu_custom_call" | custom-call | tf_op jit(solution)/shard_map/attention/pallas_call | solution.py:482
  87.8 4.0 %deliver.1 = (bf16[256,16,128]{2,1,0:T(8,128)(2,1)}, bf16[256,16,128]{2,1,0:T(8,128)(2,1)}, bf16[256,8,128]{2,1,0:T(8,128)(2,1)}, bf16[256,8,128]{2,1,0:T(8,128)...) custom-call(bf16[256,16,128]{2,1,0:T(8,128)(2,1)} %get-tuple-element.17.o, bf16[256,16,128]{2,1,0:T(8,128)(2,1)} %get-tuple-element.18.dq, ...), custom_call_target="tpu_custom_call" | custom-call | tf_op jit(solution)/shard_map/deliver/pallas_call | solution.py:577
